TPU v7x, 512 devices: a whole 4x4x16 slice. The times are simulated.
512 devices in a mesh: ctx: 32 (over y, x, core), head: 16 (over z).
Axes of the slice: x: 4, y: 4, z: 16, core: 2. Of those that a mesh axis runs over, the one named last changes fastest.
Arguments:
- queries: bfloat16 [16384, 8192], P('ctx', 'head'), may hold values from -6 to 6
- keys: bfloat16 [16384, 8192], P('ctx', 'head'), may hold values from -0.59765625 to 0.59765625
- values: bfloat16 [16384, 8192], P('ctx', 'head'), may hold values from -6 to 6
- log_decay: float32 [16384, 64], P('ctx', 'head'), may hold values from -0.76 to 0, as said below
- gain: float32 [8192], P('head'), may hold values from 0.1 to 1.9
- upstream: bfloat16 [16384, 8192], P('ctx', 'head'), may hold values from -6 to 6
Outputs:
- grad_queries: bfloat16 [16384, 8192], P('ctx', 'head')
- grad_keys: bfloat16 [16384, 8192], P('ctx', 'head')
- grad_values: bfloat16 [16384, 8192], P('ctx', 'head')
Inputs may be any that keep to these rules, and one draw needn't show every extreme that they name: `log_decay`: the logarithm of the decay that each head applies at each token.
All inputs are finite; a program needn't handle non-finite values.
Results may differ from a plain program's by a relative error of at most 0.0054.
Values sent between devices are 32-bit elements; how exact they have to be, the bound alone decides.
No kernel may reach another device: no remote copies, remote signals or barrier semaphores. Data moves between devices by JAX's collectives and lax.ppermute only.
A program may use at most 64 MiB of HBM per device.

v0:
```python
import jax
import jax.numpy as jnp
from jax import lax
from jax.sharding import PartitionSpec as P

BLK = 512


HIGHEST = lax.Precision.HIGHEST
EPSILON = 1e-06


def decay_matrix(cumulative):
    columns = cumulative.T
    spread = columns[:, :, None] - columns[:, None, :]
    positions = jnp.arange(cumulative.shape[0])
    causal = (positions[:, None] >= positions[None, :])[None]
    return jnp.where(causal, jnp.exp(jnp.where(causal, spread, 0.0)), 0.0)


def slab_weights(levels, own_index, later):
    positions = jnp.arange(levels.shape[0])
    source = positions[:, None]
    central_segment = positions[None, :]
    if later:
        between = (central_segment < source) & (central_segment > own_index)
        wanted = positions > own_index
    else:
        between = (central_segment > source) & (central_segment < own_index)
        wanted = positions < own_index
    span_sums = jnp.dot(between.astype(jnp.float32), levels, precision=HIGHEST)
    return jnp.where(wanted[:, None], jnp.exp(span_sums), 0.0)


def fold_blocks(running, segment_members):
    level_sum, summary = running
    block_total, block_state = segment_members
    return (
        (level_sum + block_total, jnp.exp(block_total)[:, None, None] * summary + block_state),
        None,
    )


def on_device(queries, keys, values, log_decay, gain, upstream):
    token_count = queries.shape[0]
    head_count = log_decay.shape[1]
    width_per_head = queries.shape[1] // head_count
    full_width = queries.shape[1] * lax.axis_size("head")
    block_count = token_count // BLK
    block_shape = (block_count, BLK, head_count, width_per_head)
    query_blocks = queries.reshape(block_shape)
    key_blocks = keys.reshape(block_shape)
    value_blocks = values.reshape(block_shape)
    cumulative = jnp.cumsum(log_decay.reshape(block_count, BLK, head_count), axis=1)
    totals = cumulative[:, -1, :]
    ending = jnp.exp(totals[:, None, :] - cumulative)
    weighted_keys = (key_blocks.astype(jnp.float32) * ending[..., None]).astype(jnp.bfloat16)
    block_states = jnp.einsum(
        "nbhe,nbhf->nhef", weighted_keys, value_blocks, preferred_element_type=jnp.float32
    )
    blank_level_start = jnp.zeros((head_count,), jnp.float32)
    empty_state = jnp.zeros((head_count, width_per_head, width_per_head), jnp.float32)
    (slab_level, slab_state), _ = lax.scan(
        fold_blocks, (blank_level_start, empty_state), (totals, block_states)
    )
    own_index = lax.axis_index("ctx")
    levels, states = (
        lax.all_gather(slab_level[None], "ctx", axis=0, tiled=True),
        lax.all_gather(slab_state[None], "ctx", axis=0, tiled=True),
    )
    weights = slab_weights(levels, own_index, False)
    start_state = jnp.einsum("nh,nhef->hef", weights, states, precision=HIGHEST)

    def forward_block(carried_over_state, segment_members):
        query_block, key_block, value_block, cum_block, total_block, state_block = segment_members
        decays = decay_matrix(cum_block)
        carried = (
            jnp.einsum(
                "the,hef->thf",
                query_block.astype(jnp.float32),
                carried_over_state,
                precision=HIGHEST,
            )
            * jnp.exp(cum_block)[:, :, None]
        )
        scores = jnp.einsum(
            "the,she->hts", query_block, key_block, preferred_element_type=jnp.float32
        )
        mixing = (scores * decays).astype(jnp.bfloat16)
        attended = carried + jnp.einsum(
            "hts,shf->thf", mixing, value_block, preferred_element_type=jnp.float32
        )
        new_state = jnp.exp(total_block)[:, None, None] * carried_over_state + state_block
        return (new_state, (attended, carried_over_state))

    _, (attended_all, opening_indices) = lax.scan(
        forward_block,
        start_state,
        (query_blocks, key_blocks, value_blocks, cumulative, totals, block_states),
    )
    attended = attended_all.reshape(token_count, -1)
    scaled_grad = gain * upstream.astype(jnp.float32)
    square_sum, mutual_accumulation = lax.psum(
        (jnp.sum(attended * attended, axis=1), jnp.sum(scaled_grad * attended, axis=1)), "head"
    )
    inverse = lax.rsqrt(square_sum / full_width + EPSILON)
    grad_out = (
        inverse[:, None] * scaled_grad
        - attended * (inverse * inverse * inverse * mutual_accumulation / full_width)[:, None]
    ).astype(jnp.bfloat16)
    grad_blocks = grad_out.reshape(block_shape)
    weighted_queries = (query_blocks.astype(jnp.float32) * jnp.exp(cumulative)[..., None]).astype(
        jnp.bfloat16
    )
    block_grads = jnp.einsum(
        "nbhe,nbhf->nhef", weighted_queries, grad_blocks, preferred_element_type=jnp.float32
    )
    (back_level, slab_grad), _ = lax.scan(
        fold_blocks, (blank_level_start, empty_state), (totals, block_grads), reverse=True
    )
    back_levels, back_states = (
        lax.all_gather(back_level[None], "ctx", axis=0, tiled=True),
        lax.all_gather(slab_grad[None], "ctx", axis=0, tiled=True),
    )
    back_weights = slab_weights(back_levels, own_index, True)
    end_state = jnp.einsum("nh,nhef->hef", back_weights, back_states, precision=HIGHEST)

    def backward_block(after_state, segment_members):
        (
            query_block,
            key_block,
            value_block,
            grad_block,
            cum_block,
            total_block,
            grad_state,
            start_block,
        ) = segment_members
        decays = decay_matrix(cum_block)
        ending_block = jnp.exp(total_block[None, :] - cum_block)[:, :, None]
        scores = jnp.einsum(
            "the,she->hts", query_block, key_block, preferred_element_type=jnp.float32
        )
        mixing = (scores * decays).astype(jnp.bfloat16)
        grad_scores = jnp.einsum(
            "thf,shf->hts", grad_block, value_block, preferred_element_type=jnp.float32
        )
        grad_mixing = (grad_scores * decays).astype(jnp.bfloat16)
        grad_query = (
            jnp.einsum(
                "thf,hef->the", grad_block.astype(jnp.float32), start_block, precision=HIGHEST
            )
            * jnp.exp(cum_block)[:, :, None]
        )
        grad_query = grad_query + jnp.einsum(
            "hts,she->the", grad_mixing, key_block, preferred_element_type=jnp.float32
        )
        grad_key = (
            jnp.einsum(
                "shf,hef->she", value_block.astype(jnp.float32), after_state, precision=HIGHEST
            )
            * ending_block
        )
        grad_key = grad_key + jnp.einsum(
            "hts,the->she", grad_mixing, query_block, preferred_element_type=jnp.float32
        )
        grad_value = (
            jnp.einsum(
                "she,hef->shf", key_block.astype(jnp.float32), after_state, precision=HIGHEST
            )
            * ending_block
        )
        grad_value = grad_value + jnp.einsum(
            "hts,thf->shf", mixing, grad_block, preferred_element_type=jnp.float32
        )
        before_state = jnp.exp(total_block)[:, None, None] * after_state + grad_state
        return (
            before_state,
            (
                grad_query.astype(jnp.bfloat16),
                grad_key.astype(jnp.bfloat16),
                grad_value.astype(jnp.bfloat16),
            ),
        )

    _, (grad_q_all, grad_k_all, grad_v_all) = lax.scan(
        backward_block,
        end_state,
        (
            query_blocks,
            key_blocks,
            value_blocks,
            grad_blocks,
            cumulative,
            totals,
            block_grads,
            opening_indices,
        ),
        reverse=True,
    )
    return (
        grad_q_all.reshape(token_count, -1),
        grad_k_all.reshape(token_count, -1),
        grad_v_all.reshape(token_count, -1),
    )


def solution(mesh):
    placed = (
        P("ctx", "head"),
        P("ctx", "head"),
        P("ctx", "head"),
        P("ctx", "head"),
        P("head"),
        P("ctx", "head"),
    )
    return jax.shard_map(
        on_device,
        mesh=mesh,
        in_specs=placed,
        out_specs=(P("ctx", "head"), P("ctx", "head"), P("ctx", "head")),
        check_vma=False,
    )
```

profile of v0, /device:TPU:1, one launch (start us, length us, event | category | flops | bytes accessed | tf_op | source)
XLA Modules:
  0.0 221.6 jit_solution(14152143247083747754)
XLA Ops:
  7.2 0.8 reshape.187
  8.0 1.2 reduce-window.6
  10.0 1.3 copy.197
  11.3 1.0 convolution_add_fusion.1
  12.4 1.3 copy.165
  13.7 24.1 %all-gather = f32[32,1,4]{2,1,0:T(1,128)S(1)} all-gather(f32[1,1,4]{2,1,0:T(1,128)S(1)} %copy.130), channel_id=2, replica_groups=mesh['ctx'=32,'head'=16] {'ctx'}, dimensions={0}, use_global_device_ids=true | all-gather | bytes 528 | tf_op jit(solution)/shard_map/all_gather | solution.py:68
  37.9 0.2 fusion.16
  38.1 1.6 multiply_convert_fusion.1
  39.7 1.3 copy-done.1
  41.1 0.8 convolution_bitcast_fusion.3
  41.9 44.5 %all-gather.6.cloned.1.call-done = f32[128,128,128]{2,1,0:T(8,128)} async-done(((f32[4,128,128]{2,1,0:T(8,128)}), f32[128,128,128]{2,1,0:T(8,128)}) %all-gather.6.cloned.1.call-update) | async-done | bytes 8388624 | tf_op jit(solution)/shard_map/all_gather | solution.py:69
  86.4 12.0 %fusion.2 = f32[4,1,128,128]{3,1,2,0:T(1,128)S(1)} fusion(f32[32,4,1,1]{0,2,3,1:T(1,128)S(1)} %bitcast.164, f32[32,4,128,128]{3,2,1,0:T(8,128)} %bitcast.142), kind=kOutput, calls=%fused_computation.2 | convolution fusion | flops 25165824 | bytes 8651264 | tf_op jit(solution)/shard_map/nh,nhef->hef/dot_general | solution.py:72
  98.4 0.7 multiply_reduce_fusion.1
  99.1 0.3 copy.140
  99.5 1.3 multiply_reduce_fusion
  100.8 24.9 %all-reduce = (f32[512]{0:T(512)S(1)}, f32[512]{0:T(512)S(1)}) all-reduce(f32[512]{0:T(512)S(1)} %multiply_reduce_fusion, f32[512]{0:T(512)S(1)} %get-tuple-element.114), channel_id=1, replica_groups=mesh['ctx'=32,'head'=16] {'head'}, use_global_device_ids=true, to_apply=%region_5.6 | all-reduce | flops 1024 | bytes 8192 | tf_op jit(solution)/shard_map/psum | solution.py:103
  125.7 1.3 subtract_convert_fusion
  127.0 0.2 copy.166
  127.2 1.0 convolution_add_fusion
  128.5 1.5 multiply_convert_fusion
  130.0 1.3 copy-done.3
  131.4 0.8 convolution_bitcast_fusion.2
  132.2 2.4 %fusion.12 = bf16[512,4,128]{0,2,1:T(8,128)(2,1)} fusion(f32[512,4,128]{0,2,1:T(8,128)S(1)} %convolution_bitcast_fusion.2, f32[4,128,128]{2,1,0:T(8,128)S(1)} %bitcast.150, bf16[512,4,128]{0,2,1:T(8,128)(2,1)} %bitcast.146, f32[512,4]{0,1:T(4,128)S(1)} %get-tuple-element.109), kind=kOutput, calls=%fused_computation.23 | convolution fusion | flops 403439616 | bytes 2367488 | tf_op jit(solution)/shard_map/while/body/eval_jaxpr/thf,hef->the/dot_general | solution.py:150
  134.6 2.0 copy.152
  136.7 2.7 %convolution_bitcast_fusion.1 = f32[512,4,128]{0,2,1:T(8,128)} fusion(bf16[512,4,128]{0,2,1:T(8,128)(2,1)} %bitcast.147, bf16[4,512,512]{2,1,0:T(8,128)(2,1)S(1)} %copy-done.2), kind=kOutput, calls=%fused_computation.8 | convolution fusion | flops 268435456 | bytes 3670016 | tf_op jit(solution)/shard_map/while/body/eval_jaxpr/hts,thf->shf/dot_general | solution.py:173
  139.4 0.4 convolution_bitcast_fusion
  139.8 59.5 %all-gather.8.cloned.1.call-done = f32[128,128,128]{2,1,0:T(8,128)} async-done(((f32[4,128,128]{2,1,0:T(8,128)}), f32[128,128,128]{2,1,0:T(8,128)}) %all-gather.8.cloned.1.call-update) | async-done | bytes 8388624 | tf_op jit(solution)/shard_map/all_gather | solution.py:123
  199.3 12.1 %fusion = f32[4,1,128,128]{3,1,2,0:T(1,128)S(1)} fusion(f32[32,4,1,1]{0,2,3,1:T(1,128)S(1)} %bitcast.163, f32[32,4,128,128]{3,2,1,0:T(8,128)} %bitcast.143), kind=kOutput, calls=%fused_computation | convolution fusion | flops 25165824 | bytes 8651264 | tf_op jit(solution)/shard_map/nh,nhef->hef/dot_general | solution.py:126
  211.5 0.7 fusion.14
  212.2 1.0 copy.154
  213.2 0.6 fusion.13
  213.8 1.0 copy.153
  (46 shorter events, 1.4 us)
Async XLA Ops:
  7.2 4.1 %copy-start = (bf16[512,512]{1,0:T(8,128)(2,1)S(1)}, bf16[512,512]{1,0:T(8,128)(2,1)}, u32[]{:S(2)}) copy-start(bf16[512,512]{1,0:T(8,128)(2,1)} %param.8) | copy-start | bytes 1572868
  7.2 30.9 %copy-start.9 = (bf16[512,512]{1,0:T(8,128)(2,1)S(1)}, bf16[512,512]{1,0:T(8,128)(2,1)}, u32[]{:S(2)}) copy-start(bf16[512,512]{1,0:T(8,128)(2,1)} %param.7) | copy-start | bytes 1572868
  7.2 79.2 %all-gather.6.cloned.1.call-start = ((), (), s32[]{:S(2)}) async-start(), calls=%async_computation | async-start | bytes 8650752 | tf_op jit(solution)/shard_map/all_gather | solution.py:69
  11.2 1.1 copy-start.7
  12.3 187.0 %all-gather.8.cloned.1.call-start = ((), (), s32[]{:S(2)}) async-start(), calls=%async_computation.1 | async-start | bytes 8650752 | tf_op jit(solution)/shard_map/all_gather | solution.py:123
  37.8 1.9 copy-start.11
  39.7 1.4 copy-start.1
  98.4 1.1 copy-start.13
  99.5 29.0 %copy-start.12 = (pred[512,512]{1,0:T(8,128)(4,1)S(1)}, pred[512,512]{1,0:T(8,128)(4,1)}, u32[]{:S(2)}) copy-start(pred[512,512]{1,0:T(8,128)(4,1)} %copy-done.11) | copy-start | bytes 786436
  127.2 1.2 copy-start.5
  128.5 2.9 %copy-start.8 = (bf16[512,512]{0,1:T(8,128)(2,1)S(1)}, bf16[512,512]{0,1:T(8,128)(2,1)}, u32[]{:S(2)}) copy-start(bf16[512,512]{0,1:T(8,128)(2,1)} %copy-done.7) | copy-start | bytes 1572868
  130.0 1.3 copy-start.3
  131.4 5.3 %copy-start.2 = (bf16[4,512,512]{2,1,0:T(8,128)(2,1)S(1)}, bf16[4,512,512]{2,1,0:T(8,128)(2,1)}, u32[]{:S(2)}) copy-start(bf16[4,512,512]{2,1,0:T(8,128)(2,1)} %copy-done.1) | copy-start | bytes 6291460
  136.7 2.7 %copy-start.4 = (bf16[4,512,512]{2,1,0:T(8,128)(2,1)S(1)}, bf16[4,512,512]{2,1,0:T(8,128)(2,1)}, u32[]{:S(2)}) copy-start(bf16[4,512,512]{2,1,0:T(8,128)(2,1)} %copy-done.3) | copy-start | bytes 6291460
  199.3 12.1 %copy-start.6 = (f32[512,4,128]{0,2,1:T(8,128)S(1)}, f32[512,4,128]{0,2,1:T(8,128)}, u32[]{:S(2)}) copy-start(f32[512,4,128]{0,2,1:T(8,128)} %convolution_bitcast_fusion.1) | copy-start | bytes 3145732
  199.3 12.2 %copy-start.10 = (bf16[512,512]{1,0:T(8,128)(2,1)S(1)}, bf16[512,512]{1,0:T(8,128)(2,1)}, u32[]{:S(2)}) copy-start(bf16[512,512]{1,0:T(8,128)(2,1)} %param.7) | copy-start | bytes 1572868
Sparse Core Ops, SparseCore 0:
  12.4 73.9 all-gather.5
  128.4 70.8 all-gather.7
where the time goes:
time: 222 us
  waiting for transfers between devices  104 us (47%)
  blocking collectives  49 us (22%)
  matrix products  38.8 us (17%)
  between operations  14.3 us (6%)
  local copies, waits for them, and re-layouts  11.2 us (5%)
  other arithmetic  4.22 us (2%)
    all_gather x1, waiting for transfers between devices, on_device(): lax.all_gather(slab_grad[None], 'ctx', axis=0, tiled=True)  59.5 us
    all_gather x1, waiting for transfers between devices, on_device(): lax.all_gather(slab_state[None], 'ctx', axis=0, tiled=True)  44.5 us
    psum x1, blocking collectives, on_device(): lax.psum((jnp.sum(attended * attended, axis=1), jnp.sum(scaled_grad * att...  24.9 us
    all_gather x1, blocking collectives, on_device(): lax.all_gather(slab_level[None], 'ctx', axis=0, tiled=True)  24.1 us
    dot_general x1, matrix products, on_device(): jnp.einsum('nh,nhef->hef', back_weights, back_states, precision=HIGHEST)  12.1 us
    dot_general x1, matrix products, on_device(): start_state = jnp.einsum('nh,nhef->hef', weights, states, precision=HIGHEST)  12 us
    unnamed x31, local copies, waits for them, and re-layouts  6.81 us
  transfers between devices with their start and end apart: 2, of which 2 were waited for; matrix products, arithmetic and copies ran while one was open for 6% of the time, Pallas kernels for 0%

commit v1 on v0

v1 whole, which is shorter than its diff:
```python
import functools

import jax
import jax.numpy as jnp
from jax import lax
from jax.experimental import pallas as pl
from jax.experimental.pallas import tpu as pltpu
from jax.sharding import PartitionSpec as P

HEAD_DIM = 128
BLK = 512
TILE = 128
HALF = 256
EPSILON = 1e-06
F32 = jnp.float32
BF16 = jnp.bfloat16
VMEM_LIMIT = 40 * 1024 * 1024


def dot(a, b, contract, precision=None):
    return lax.dot_general(
        a, b, (((contract[0],), (contract[1],)), ((), ())),
        precision=precision, preferred_element_type=F32,
    )


def head_cols(h):
    return slice(h * HEAD_DIM, (h + 1) * HEAD_DIM)


def split(x):
    high = x.astype(BF16)
    return high, (x - high.astype(F32)).astype(BF16)


def twice(x):
    return jnp.concatenate([x, x], axis=1)


def eye():
    rows = lax.broadcasted_iota(jnp.int32, (TILE, TILE), 0)
    return rows == lax.broadcasted_iota(jnp.int32, (TILE, TILE), 1)


def decay_tile(cumulative, columns, h, start, width):
    t = start + lax.broadcasted_iota(jnp.int32, (HALF, width), 0)
    s = lax.broadcasted_iota(jnp.int32, (HALF, width), 1)
    spread = columns[start:start + HALF, h:h + 1] - cumulative[h:h + 1, :width]
    return jnp.exp(jnp.where(s <= t, spread, -1e30))


def piece_rows(devices):
    return 4 * HEAD_DIM // devices


def local_states(log_decay_ref, keys_ref, values_ref, out_ref, cum_ref):
    heads = log_decay_ref.shape[0]
    devices = out_ref.shape[0]
    rows = piece_rows(devices)
    per_head = HEAD_DIM // rows
    s = lax.broadcasted_iota(jnp.int32, (TILE, TILE), 0)
    until = (s <= lax.broadcasted_iota(jnp.int32, (TILE, TILE), 1)).astype(F32)
    parts = []
    total = jnp.zeros((heads, 1), F32)
    for j in range(BLK // TILE):
        within = dot(
            log_decay_ref[:, j * TILE:(j + 1) * TILE], until, (1, 0), lax.Precision.HIGHEST
        )
        parts.append(within + total)
        total = parts[-1][:, TILE - 1:TILE]
    cumulative = jnp.concatenate(parts, axis=1)
    ending = jnp.exp(total - cumulative)
    both = jnp.concatenate([cumulative, ending], axis=0)
    cum_ref[...] = both
    columns = both.T
    for h in range(heads):
        weighted = keys_ref[:, head_cols(h)].astype(F32) * columns[:, heads + h:heads + h + 1]
        state = dot(weighted.astype(BF16), values_ref[:, head_cols(h)], (0, 0))
        pieces = slice(h * per_head, (h + 1) * per_head)
        out_ref[pieces, :rows, :] = state.reshape(per_head, rows, HEAD_DIM)
        out_ref[pieces, rows:, :] = jnp.broadcast_to(
            total[h:h + 1].reshape(1, 1, 1), (per_head, 8, HEAD_DIM)
        )


def prefix(members_ref, out_ref):
    devices, rows = out_ref.shape[:2]
    running = jnp.zeros((rows, HEAD_DIM), F32)
    for b in range(devices):
        out_ref[b] = running
        if b < devices - 1:
            decay = jnp.exp(members_ref[b, rows:rows + 1, :])
            running = decay * running + members_ref[b, :rows, :]


def suffix(members_ref, levels_ref, out_ref):
    devices, rows = out_ref.shape[:2]
    running = jnp.zeros((rows, HEAD_DIM), F32)
    for b in reversed(range(devices)):
        out_ref[b] = running
        if b > 0:
            decay = jnp.exp(levels_ref[b, rows:rows + 1, :])
            running = decay * running + members_ref[b]


def local_attention(queries_ref, keys_ref, values_ref, cum_ref, mixing_ref, local_ref):
    heads = mixing_ref.shape[0]
    cumulative = cum_ref[...]
    columns = cumulative.T
    for h in range(heads):
        cols = head_cols(h)
        for start in range(0, BLK, HALF):
            width = start + HALF
            scores = dot(queries_ref[start:width, cols], keys_ref[:width, cols], (1, 1))
            mixing = (scores * decay_tile(cumulative, columns, h, start, width)).astype(BF16)
            mixing_ref[h, start:width, :width] = mixing
            local_ref[start:width, cols] = dot(mixing, values_ref[:width, cols], (1, 0))


def attend(queries_ref, upstream_ref, gain_ref, cum_ref, local_ref, state_ref, att_ref, sums_ref):
    heads = state_ref.shape[0]
    columns = jnp.exp(cum_ref[...]).T
    square = jnp.zeros((BLK, HEAD_DIM), F32)
    cross = jnp.zeros((BLK, HEAD_DIM), F32)
    for h in range(heads):
        cols = head_cols(h)
        high, low = split(state_ref[h])
        carried = dot(twice(queries_ref[:, cols]), jnp.concatenate([high, low], axis=0), (1, 0))
        attended = local_ref[:, cols] + columns[:, h:h + 1] * carried
        att_ref[:, cols] = attended
        scaled = gain_ref[:, cols] * upstream_ref[:, cols].astype(F32)
        square = square + attended * attended
        cross = cross + scaled * attended
    same = eye()
    rows = []
    for summed in (square, cross):
        for j in range(BLK // TILE):
            column = jnp.sum(summed[j * TILE:(j + 1) * TILE], axis=1, keepdims=True)
            rows.append(jnp.sum(jnp.where(same, column, 0.0), axis=0, keepdims=True))
    sums = jnp.concatenate(rows, axis=0)
    for d in range(sums_ref.shape[0]):
        sums_ref[d] = sums


def grad_states(width, sums_ref, att_ref, upstream_ref, gain_ref, queries_ref, cum_ref, grad_ref, out_ref):
    devices = out_ref.shape[0]
    rows = piece_rows(devices)
    per_head = HEAD_DIM // rows
    heads = devices // per_head
    sums = jnp.sum(sums_ref[...], axis=0)
    tiles = BLK // TILE
    inverse = lax.rsqrt(sums[:tiles] / width + EPSILON)
    pull = inverse * inverse * inverse * sums[tiles:] / width
    scales = jnp.concatenate([inverse, pull], axis=0).T
    columns = jnp.exp(cum_ref[...]).T
    for h in range(heads):
        cols = head_cols(h)
        for j in range(tiles):
            part = slice(j * TILE, (j + 1) * TILE)
            scaled = gain_ref[:, cols] * upstream_ref[part, cols].astype(F32)
            grad = scales[:, j:j + 1] * scaled - att_ref[part, cols] * scales[:, tiles + j:tiles + j + 1]
            grad_ref[part, cols] = grad.astype(BF16)
        weighted = queries_ref[:, cols].astype(F32) * columns[:, h:h + 1]
        state = dot(weighted.astype(BF16), grad_ref[:, cols], (0, 0))
        out_ref[h * per_head:(h + 1) * per_head] = state.reshape(per_head, rows, HEAD_DIM)


def local_grads(
    queries_ref, keys_ref, values_ref, grad_ref, cum_ref, state_ref, mixing_ref,
    grad_queries_ref, grad_keys_ref, grad_values_ref,
):
    heads = state_ref.shape[0]
    cumulative = cum_ref[...]
    columns = cumulative.T
    for h in range(heads):
        cols = head_cols(h)
        high, low = split(state_ref[h])
        both = jnp.concatenate([high, low], axis=1)
        for start in range(0, BLK, HALF):
            width = start + HALF
            grad = grad_ref[start:width, cols]
            scores = dot(grad, values_ref[:width, cols], (1, 1))
            mixing = (scores * decay_tile(cumulative, columns, h, start, width)).astype(BF16)
            carried = dot(twice(grad), both, (1, 1))
            grad_query = jnp.exp(columns[start:width, h:h + 1]) * carried
            grad_query = grad_query + dot(mixing, keys_ref[:width, cols], (1, 0))
            grad_queries_ref[start:width, cols] = grad_query.astype(BF16)
            grad_key = dot(mixing, queries_ref[start:width, cols], (0, 0))
            grad_value = dot(mixing_ref[h, start:width, :width], grad, (0, 0))
            if start == 0:
                grad_keys_ref[:width, cols] = grad_key
                grad_values_ref[:width, cols] = grad_value
            else:
                grad_keys_ref[:start, cols] += grad_key[:start]
                grad_values_ref[:start, cols] += grad_value[:start]
                grad_keys_ref[start:width, cols] = grad_key[start:]
                grad_values_ref[start:width, cols] = grad_value[start:]


def add_carried(
    keys_ref, values_ref, cum_ref, state_ref, local_keys_ref, local_values_ref,
    grad_keys_ref, grad_values_ref,
):
    heads = state_ref.shape[0]
    columns = cum_ref[...].T
    for h in range(heads):
        cols = head_cols(h)
        high, low = split(state_ref[h])
        ending = columns[:, heads + h:heads + h + 1]
        grad_key = dot(twice(values_ref[:, cols]), jnp.concatenate([high, low], axis=1), (1, 1))
        grad_value = dot(twice(keys_ref[:, cols]), jnp.concatenate([high, low], axis=0), (1, 0))
        grad_keys_ref[:, cols] = (local_keys_ref[:, cols] + ending * grad_key).astype(BF16)
        grad_values_ref[:, cols] = (local_values_ref[:, cols] + ending * grad_value).astype(BF16)


def call(kernel, name, out_shape, *args, flops=0):
    outs = jax.tree.leaves(out_shape)
    size = sum(a.size * a.dtype.itemsize for a in (*args, *outs))
    return pl.pallas_call(
        kernel,
        out_shape=out_shape,
        name=name,
        compiler_params=pltpu.CompilerParams(vmem_limit_bytes=VMEM_LIMIT),
        cost_estimate=pl.CostEstimate(flops=flops, bytes_accessed=size, transcendentals=0),
    )(*args)


def on_device(queries, keys, values, log_decay, gain, upstream):
    tokens, columns = queries.shape
    heads = log_decay.shape[1]
    slabs = lax.axis_size("ctx")
    groups = lax.axis_size("head")
    rows = piece_rows(slabs)
    full_width = columns * groups
    gain = gain[None]
    f32 = functools.partial(jax.ShapeDtypeStruct, dtype=F32)
    bf16 = functools.partial(jax.ShapeDtypeStruct, dtype=BF16)
    square = tokens * tokens * HEAD_DIM * heads * 2

    def exchange(x, axis):
        return lax.all_to_all(x, axis, 0, 0, tiled=True)

    pieces, cumulative = call(
        local_states, "local_states", (f32((slabs, rows + 8, HEAD_DIM)), f32((2 * heads, tokens))),
        log_decay.T, keys, values, flops=square // 4,
    )
    members = exchange(pieces, "ctx")
    mixing, local = call(
        local_attention, "local_attention",
        (bf16((heads, tokens, tokens)), f32((tokens, columns))),
        queries, keys, values, cumulative, flops=2 * square,
    )
    starts = call(prefix, "prefix", f32((slabs, rows, HEAD_DIM)), members)
    start_state = exchange(starts, "ctx").reshape(heads, HEAD_DIM, HEAD_DIM)
    attended, sums = call(
        attend, "attend", (f32((tokens, columns)), f32((groups, 2 * tokens // TILE, TILE))),
        queries, upstream, gain, cumulative, local, start_state, flops=square // 2,
    )
    sums = exchange(sums, "head")
    grad_out, grad_pieces = call(
        functools.partial(grad_states, full_width), "grad_states",
        (bf16((tokens, columns)), f32((slabs, rows, HEAD_DIM))),
        sums, attended, upstream, gain, queries, cumulative, flops=square // 4,
    )
    grad_members = exchange(grad_pieces, "ctx")
    grad_queries, local_keys, local_values = call(
        local_grads, "local_grads",
        (bf16((tokens, columns)), f32((tokens, columns)), f32((tokens, columns))),
        queries, keys, values, grad_out, cumulative, start_state, mixing, flops=4 * square,
    )
    ends = call(suffix, "suffix", f32((slabs, rows, HEAD_DIM)), grad_members, members)
    end_state = exchange(ends, "ctx").reshape(heads, HEAD_DIM, HEAD_DIM)
    grad_keys, grad_values = call(
        add_carried, "add_carried", (bf16((tokens, columns)), bf16((tokens, columns))),
        keys, values, cumulative, end_state, local_keys, local_values, flops=square,
    )
    return grad_queries, grad_keys, grad_values


def solution(mesh):
    placed = (
        P("ctx", "head"),
        P("ctx", "head"),
        P("ctx", "head"),
        P("ctx", "head"),
        P("head"),
        P("ctx", "head"),
    )
    return jax.shard_map(
        on_device,
        mesh=mesh,
        in_specs=placed,
        out_specs=(P("ctx", "head"), P("ctx", "head"), P("ctx", "head")),
        check_vma=False,
    )
```

time: 222 us -> 98.7 us (0.44)
  waiting for transfers between devices: 104 us -> 6.58 us
  matrix products: 38.8 us -> 0 us
  between operations: 14.3 us -> 0.76 us
  Pallas kernels: 0 us -> 11.9 us
  blocking collectives: 49 us -> 59.2 us
  starting transfers between devices: 0.08 us -> 7.65 us
  other arithmetic: 4.22 us -> 0 us
    all_gather x2 -> x0, waiting for transfers between devices: 104 us -> none  [the longest x1 59.5 us: on_device(): lax.all_gather(slab_grad[None], 'ctx', axis=0, tiled=True)]
    all_to_all x0 -> x3, blocking collectives: none -> 59.2 us  [exchange(): return lax.all_to_all(x, axis, 0, 0, tiled=True)]
    dot_general x16 -> x0, matrix products: 38.8 us -> none  [the longest x1 12.1 us: on_device(): jnp.einsum('nh,nhef->hef', back_weights, back_states, precision=HIGHEST)]
    psum x1 -> x0, blocking collectives: 24.9 us -> none  [on_device(): lax.psum((jnp.sum(attended * attended, axis=1), jnp.sum(scaled_grad * att...]
    all_gather x1 -> x0, blocking collectives: 24.1 us -> none  [on_device(): lax.all_gather(slab_level[None], 'ctx', axis=0, tiled=True)]
    pallas_call x0 -> x8, Pallas kernels: none -> 11.9 us  [call(): pl.pallas_call(kernel, out_shape=out_shape, name=name, compiler_params=pl...]
    all_to_all x0 -> x2, starting transfers between devices: none -> 7.65 us  [exchange(): return lax.all_to_all(x, axis, 0, 0, tiled=True)]
    all_to_all x0 -> x2, waiting for transfers between devices: none -> 6.58 us  [exchange(): return lax.all_to_all(x, axis, 0, 0, tiled=True)]
  transfers between devices with their start and end apart: 2 -> 2, of which waited for: 2 -> 2; matrix products, arithmetic and copies ran while one was open for 6% -> 0% of each run, Pallas kernels for 0% -> 6%
where the time goes in v1:
time: 98.7 us; the launch traced here: 98.1 us
  blocking collectives  59.2 us (60%)
  local copies, waits for them, and re-layouts  12 us (12%)
  Pallas kernels  11.9 us (12%)
  starting transfers between devices  7.65 us (8%)
  waiting for transfers between devices  6.58 us (7%)
    all_to_all x3, blocking collectives, exchange(): return lax.all_to_all(x, axis, 0, 0, tiled=True)  59.2 us
    unnamed x32, local copies, waits for them, and re-layouts  12 us
    pallas_call x8, Pallas kernels, call(): pl.pallas_call(kernel, out_shape=out_shape, name=name, compiler_params=pl...  11.9 us
    all_to_all x2, starting transfers between devices, exchange(): return lax.all_to_all(x, axis, 0, 0, tiled=True)  7.65 us
    all_to_all x2, waiting for transfers between devices, exchange(): return lax.all_to_all(x, axis, 0, 0, tiled=True)  6.58 us
  transfers between devices with their start and end apart: 2, of which 2 were waited for; matrix products, arithmetic and copies ran while one was open for 0% of the time, Pallas kernels for 6%

profile of v1, /device:TPU:1, one launch (start us, length us, event | category | flops | bytes accessed | tf_op | source)
XLA Modules:
  0.0 98.1 jit_solution(2423071055268876151)
XLA Ops:
  0.6 0.0 copy-start
  0.7 1.1 %copy-done.1 = bf16[512,512]{1,0:T(8,128)(2,1)S(1)} copy-done((bf16[512,512]{1,0:T(8,128)(2,1)S(1)}, bf16[512,512]{1,0:T(8,128)(2,1)}, u32[]{:S(2)}) %copy-start.1) | copy-done | bytes 524312
  1.7 1.0 %copy-done.3 = bf16[512,512]{1,0:T(8,128)(2,1)S(1)} copy-done((bf16[512,512]{1,0:T(8,128)(2,1)S(1)}, bf16[512,512]{1,0:T(8,128)(2,1)}, u32[]{:S(2)}) %copy-start.3) | copy-done | bytes 524312
  2.8 0.7 copy-done.14
  3.5 1.3 %local_states.1 = (f32[32,24,128]{2,1,0:T(8,128)S(1)}, f32[8,512]{1,0:T(8,128)S(1)}) custom-call(f32[4,512]{1,0:T(4,128)S(1)} %bitcast.7, bf16[512,512]{1,0:T(8,128)(2,1)S(1)} %copy-done.1, bf16[512,512]{1,0:T(8,128)(2,1)S(1)} %copy-done.3), custom_call_target="tpu_custom_call" | custom-call | flops 67108864 | bytes 1466368 | tf_op jit(solution)/shard_map/local_states/pallas_call | solution.py:219
  4.8 0.0 copy-start.7
  4.8 0.0 copy-start.15
  4.8 19.9 %all_to_all.25.members_ref.levels_ref = f32[32,24,128]{2,1,0:T(8,128)S(1)} all-to-all(f32[32,24,128]{2,1,0:T(8,128)S(1)} %get-tuple-element.18), channel_id=1, replica_groups=mesh['ctx'=32,'head'=16] {'ctx'}, dimensions={0} | all-to-all | bytes 786432 | tf_op jit(solution)/shard_map/all_to_all | solution.py:241
  24.7 0.8 prefix.1
  25.5 3.9 %all-to-all-start.1 = ((f32[32,16,128]{2,1,0:T(8,128)}), f32[32,16,128]{2,1,0:T(8,128)S(1)}, u32[]{:S(2)}, u32[]{:S(2)}) async-start(f32[32,16,128]{2,1,0:T(8,128)} %prefix.1), calls=%async_computation.1 | async-start | bytes 524288 | tf_op jit(solution)/shard_map/all_to_all | solution.py:241
  29.5 1.7 %local_attention.1 = (bf16[4,512,512]{2,1,0:T(8,128)(2,1)S(1)}, f32[512,512]{1,0:T(8,128)S(1)}) custom-call(bf16[512,512]{1,0:T(8,128)(2,1)S(1)} %copy-done, bf16[512,512]{1,0:T(8,128)(2,1)S(1)} %copy-done.2, bf16[512,512]{1,0:T(8,128)(2,1)S(1)} %copy-done.4, f32[8,512]{1,0:T(8,128)S(1)} %get-tuple-element.16.cum_ref), custom_call_target="tpu_custom_call" | custom-call | flops 536870912 | bytes 4734976 | tf_op jit(solution)/shard_map/local_attention/pallas_call | solution.py:219
  31.1 1.3 %copy-done.5 = bf16[4,512,512]{2,1,0:T(8,128)(2,1)} copy-done((bf16[4,512,512]{2,1,0:T(8,128)(2,1)}, bf16[4,512,512]{2,1,0:T(8,128)(2,1)S(1)}, u32[]{:S(2)}) %copy-start.5) | copy-done | bytes 2097176
  32.5 1.0 %copy-done.10 = f32[512,512]{1,0:T(8,128)} copy-done((f32[512,512]{1,0:T(8,128)}, f32[512,512]{1,0:T(8,128)S(1)}, u32[]{:S(2)}) %copy-start.10) | copy-done | bytes 1048600
  33.4 5.0 %all-to-all-done.1 = f32[32,16,128]{2,1,0:T(8,128)S(1)} async-done(((f32[32,16,128]{2,1,0:T(8,128)}), f32[32,16,128]{2,1,0:T(8,128)S(1)}, u32[]{:S(2)}, u32[]{:S(2)}) %all-to-all-start.1) | async-done | bytes 262176 | tf_op jit(solution)/shard_map/all_to_all | solution.py:241
  38.4 0.0 copy-done.15
  38.4 1.2 %copy-done.11 = f32[512,512]{1,0:T(8,128)S(1)} copy-done((f32[512,512]{1,0:T(8,128)S(1)}, f32[512,512]{1,0:T(8,128)}, u32[]{:S(2)}) %copy-start.11) | copy-done | bytes 1048600
  39.7 0.8 attend.1
  40.4 25.1 %all_to_all.26.sums_ref = f32[16,8,128]{2,1,0:T(8,128)S(1)} all-to-all(f32[16,8,128]{2,1,0:T(8,128)S(1)} %get-tuple-element.19), channel_id=1, replica_groups=mesh['ctx'=32,'head'=16] {'head'}, dimensions={0} | all-to-all | bytes 131072 | tf_op jit(solution)/shard_map/all_to_all | solution.py:241
  65.5 1.1 %grad_states.1 = (bf16[512,512]{1,0:T(8,128)(2,1)S(1)}, f32[32,16,128]{2,1,0:T(8,128)S(1)}) custom-call(f32[16,8,128]{2,1,0:T(8,128)S(1)} %all_to_all.26.sums_ref, f32[512,512]{1,0:T(8,128)S(1)} %get-tuple-element.20.att_ref, bf16[512,512]{1,0:T(8,128)(2,1)S(1)} %copy-done.7, f32[1,512]{1,0:T(1,128)S(1)} %bitcast.9, bf16[512,512]{1,0:T(8,128)(2,1)S(1)} %copy-done, ...), custom_call_target="tpu_custom_call" | custom-call | flops 67108864 | bytes 2967552 | tf_op jit(solution)/shard_map/grad_states/pallas_call | solution.py:219
  66.6 0.0 copy-start.12
  66.6 0.8 copy-done.12
  67.4 14.2 %all_to_all.27.members_ref = f32[32,16,128]{2,1,0:T(8,128)S(1)} all-to-all(f32[32,16,128]{2,1,0:T(8,128)S(1)} %get-tuple-element.24), channel_id=1, replica_groups=mesh['ctx'=32,'head'=16] {'ctx'}, dimensions={0} | all-to-all | bytes 524288 | tf_op jit(solution)/shard_map/all_to_all | solution.py:241
  81.6 0.8 suffix.1
  82.4 3.8 %all-to-all-start.4 = ((f32[32,16,128]{2,1,0:T(8,128)}), f32[32,16,128]{2,1,0:T(8,128)S(1)}, u32[]{:S(2)}, u32[]{:S(2)}) async-start(f32[32,16,128]{2,1,0:T(8,128)} %suffix.1), calls=%async_computation.4 | async-start | bytes 524288 | tf_op jit(solution)/shard_map/all_to_all | solution.py:241
  86.2 0.0 copy-start.6
  86.2 1.6 %copy-done.6 = bf16[4,512,512]{2,1,0:T(8,128)(2,1)S(1)} copy-done((bf16[4,512,512]{2,1,0:T(8,128)(2,1)S(1)}, bf16[4,512,512]{2,1,0:T(8,128)(2,1)}, u32[]{:S(2)}) %copy-start.6) | copy-done | bytes 2097176
  87.8 1.0 %copy-done.13 = bf16[512,512]{1,0:T(8,128)(2,1)S(1)} copy-done((bf16[512,512]{1,0:T(8,128)(2,1)S(1)}, bf16[512,512]{1,0:T(8,128)(2,1)}, u32[]{:S(2)}) %copy-start.13) | copy-done | bytes 524312
  88.8 3.8 %local_grads.1 = (bf16[512,512]{1,0:T(8,128)(2,1)}, f32[512,512]{1,0:T(8,128)S(1)}, f32[512,512]{1,0:T(8,128)S(1)}) custom-call(bf16[512,512]{1,0:T(8,128)(2,1)S(1)} %copy-done, bf16[512,512]{1,0:T(8,128)(2,1)S(1)} %copy-done.2, bf16[512,512]{1,0:T(8,128)(2,1)S(1)} %copy-done.4, bf16[512,512]{1,0:T(8,128)(2,1)S(1)} %copy-done.13, ...), custom_call_target="tpu_custom_call" | custom-call | flops 1073741824 | bytes 7094272 | tf_op jit(solution)/shard_map/local_grads/pallas_call | solution.py:219
  92.6 1.0 %copy-done.8 = f32[512,512]{1,0:T(8,128)} copy-done((f32[512,512]{1,0:T(8,128)}, f32[512,512]{1,0:T(8,128)S(1)}, u32[]{:S(2)}) %copy-start.8) | copy-done | bytes 1048600
  93.6 1.6 %all-to-all-done.4 = f32[32,16,128]{2,1,0:T(8,128)S(1)} async-done(((f32[32,16,128]{2,1,0:T(8,128)}), f32[32,16,128]{2,1,0:T(8,128)S(1)}, u32[]{:S(2)}, u32[]{:S(2)}) %all-to-all-start.4) | async-done | bytes 262176 | tf_op jit(solution)/shard_map/all_to_all | solution.py:241
  95.2 1.2 %copy-done.9 = f32[512,512]{1,0:T(8,128)S(1)} copy-done((f32[512,512]{1,0:T(8,128)S(1)}, f32[512,512]{1,0:T(8,128)}, u32[]{:S(2)}) %copy-start.9) | copy-done | bytes 1048600
  96.4 1.7 %add_carried.1 = (bf16[512,512]{1,0:T(8,128)(2,1)}, bf16[512,512]{1,0:T(8,128)(2,1)}) custom-call(bf16[512,512]{1,0:T(8,128)(2,1)S(1)} %copy-done.2, bf16[512,512]{1,0:T(8,128)(2,1)S(1)} %copy-done.4, f32[8,512]{1,0:T(8,128)S(1)} %get-tuple-element.16.cum_ref, f32[4,128,128]{2,1,0:T(8,128)S(1)} %bitcast.6, f32[512,512]{1,0:T(8,128)S(1)} %get-tuple-element.25.local_keys_ref, ...), custom_call_target="tpu_custom_call" | custom-call | flops 268435456 | bytes 4472832 | tf_op jit(solution)/shard_map/add_carried/pallas_call | solution.py:219
  (15 shorter events, 0.0 us)
Async XLA Ops:
  0.6 28.8 %copy-start = (bf16[512,512]{1,0:T(8,128)(2,1)S(1)}, bf16[512,512]{1,0:T(8,128)(2,1)}, u32[]{:S(2)}) copy-start(bf16[512,512]{1,0:T(8,128)(2,1)} %queries_ref.7) | copy-start | bytes 1572868
  0.6 1.1 %copy-start.1 = (bf16[512,512]{1,0:T(8,128)(2,1)S(1)}, bf16[512,512]{1,0:T(8,128)(2,1)}, u32[]{:S(2)}) copy-start(bf16[512,512]{1,0:T(8,128)(2,1)} %keys_ref.7) | copy-start | bytes 1572868
  1.7 1.0 %copy-start.3 = (bf16[512,512]{1,0:T(8,128)(2,1)S(1)}, bf16[512,512]{1,0:T(8,128)(2,1)}, u32[]{:S(2)}) copy-start(bf16[512,512]{1,0:T(8,128)(2,1)} %values_ref.7) | copy-start | bytes 1572868
  2.8 0.7 copy-start.14
  3.5 26.0 %copy-start.2 = (bf16[512,512]{1,0:T(8,128)(2,1)S(1)}, bf16[512,512]{1,0:T(8,128)(2,1)}, u32[]{:S(2)}) copy-start(bf16[512,512]{1,0:T(8,128)(2,1)} %keys_ref.7) | copy-start | bytes 1572868
  3.5 26.0 %copy-start.4 = (bf16[512,512]{1,0:T(8,128)(2,1)S(1)}, bf16[512,512]{1,0:T(8,128)(2,1)}, u32[]{:S(2)}) copy-start(bf16[512,512]{1,0:T(8,128)(2,1)} %values_ref.7) | copy-start | bytes 1572868
  4.8 33.6 %copy-start.7 = (bf16[512,512]{1,0:T(8,128)(2,1)S(1)}, bf16[512,512]{1,0:T(8,128)(2,1)}, u32[]{:S(2)}) copy-start(bf16[512,512]{1,0:T(8,128)(2,1)} %upstream_ref.3) | copy-start | bytes 1572868
  4.8 33.6 %copy-start.15 = (f32[512]{0:T(512)S(1)}, f32[512]{0:T(512)}, u32[]{:S(2)}) copy-start(f32[512]{0:T(512)} %param.10) | copy-start | bytes 6148
  25.5 12.9 %all-to-all-start.1 = ((f32[32,16,128]{2,1,0:T(8,128)}), f32[32,16,128]{2,1,0:T(8,128)S(1)}, u32[]{:S(2)}, u32[]{:S(2)}) async-start(f32[32,16,128]{2,1,0:T(8,128)} %prefix.1), calls=%async_computation.1 | async-start | bytes 524288 | tf_op jit(solution)/shard_map/all_to_all | solution.py:241
  31.1 1.3 %copy-start.5 = (bf16[4,512,512]{2,1,0:T(8,128)(2,1)}, bf16[4,512,512]{2,1,0:T(8,128)(2,1)S(1)}, u32[]{:S(2)}) copy-start(bf16[4,512,512]{2,1,0:T(8,128)(2,1)S(1)} %get-tuple-element.22.mixing_ref) | copy-start | bytes 6291460
  32.5 1.0 %copy-start.10 = (f32[512,512]{1,0:T(8,128)}, f32[512,512]{1,0:T(8,128)S(1)}, u32[]{:S(2)}) copy-start(f32[512,512]{1,0:T(8,128)S(1)} %get-tuple-element.17.local_ref) | copy-start | bytes 3145732
  38.4 1.2 %copy-start.11 = (f32[512,512]{1,0:T(8,128)S(1)}, f32[512,512]{1,0:T(8,128)}, u32[]{:S(2)}) copy-start(f32[512,512]{1,0:T(8,128)} %copy-done.10) | copy-start | bytes 3145732
  66.6 0.8 copy-start.12
  82.4 12.8 %all-to-all-start.4 = ((f32[32,16,128]{2,1,0:T(8,128)}), f32[32,16,128]{2,1,0:T(8,128)S(1)}, u32[]{:S(2)}, u32[]{:S(2)}) async-start(f32[32,16,128]{2,1,0:T(8,128)} %suffix.1), calls=%async_computation.4 | async-start | bytes 524288 | tf_op jit(solution)/shard_map/all_to_all | solution.py:241
  86.2 1.6 %copy-start.6 = (bf16[4,512,512]{2,1,0:T(8,128)(2,1)S(1)}, bf16[4,512,512]{2,1,0:T(8,128)(2,1)}, u32[]{:S(2)}) copy-start(bf16[4,512,512]{2,1,0:T(8,128)(2,1)} %copy-done.5) | copy-start | bytes 6291460
  87.8 1.0 %copy-start.13 = (bf16[512,512]{1,0:T(8,128)(2,1)S(1)}, bf16[512,512]{1,0:T(8,128)(2,1)}, u32[]{:S(2)}) copy-start(bf16[512,512]{1,0:T(8,128)(2,1)} %copy-done.12) | copy-start | bytes 1572868
  92.6 1.0 %copy-start.8 = (f32[512,512]{1,0:T(8,128)}, f32[512,512]{1,0:T(8,128)S(1)}, u32[]{:S(2)}) copy-start(f32[512,512]{1,0:T(8,128)S(1)} %get-tuple-element.26.local_values_ref) | copy-start | bytes 3145732
  95.2 1.2 %copy-start.9 = (f32[512,512]{1,0:T(8,128)S(1)}, f32[512,512]{1,0:T(8,128)}, u32[]{:S(2)}) copy-start(f32[512,512]{1,0:T(8,128)} %copy-done.8) | copy-start | bytes 3145732

commit v2 on v1

v2 whole, which is shorter than its diff:
```python
import functools
import math

import jax
import jax.numpy as jnp
from jax import lax
from jax.experimental import pallas as pl
from jax.experimental.pallas import tpu as pltpu
from jax.sharding import PartitionSpec as P

HEAD_DIM = 128
BLK = 512
TILE = 128
HALF = 256
EPSILON = 1e-06
F32 = jnp.float32
BF16 = jnp.bfloat16
VMEM_LIMIT = 12 * 1024 * 1024


def dot(a, b, contract, precision=None):
    return lax.dot_general(
        a, b, (((contract[0],), (contract[1],)), ((), ())),
        precision=precision, preferred_element_type=F32,
    )


def head_cols(h):
    return slice(h * HEAD_DIM, (h + 1) * HEAD_DIM)


def split(x):
    high = x.astype(BF16)
    return high, (x - high.astype(F32)).astype(BF16)


def twice(x):
    return jnp.concatenate([x, x], axis=1)


def eye():
    rows = lax.broadcasted_iota(jnp.int32, (TILE, TILE), 0)
    return rows == lax.broadcasted_iota(jnp.int32, (TILE, TILE), 1)


def causal_exp(spread, later):
    rows = lax.broadcasted_iota(jnp.int32, (HALF, HALF), 0)
    columns = lax.broadcasted_iota(jnp.int32, (HALF, HALF), 1)
    width = spread.shape[1]
    if later:
        diagonal = jnp.where(columns >= rows, spread[:, :HALF], -1e30)
        parts = [diagonal] + [spread[:, HALF:]] * (width > HALF)
    else:
        diagonal = jnp.where(columns <= rows, spread[:, width - HALF:], -1e30)
        parts = [spread[:, :width - HALF]] * (width > HALF) + [diagonal]
    return jnp.concatenate([jnp.exp(part) for part in parts], axis=1)


def piece_rows(devices):
    return 4 * HEAD_DIM // devices


def local_states(
    log_decay_hbm, keys_hbm, values_hbm, out_ref, cum_ref, log_decay_ref, keys_ref, values_ref, sems
):
    loads = []
    for i, (source, target) in enumerate(
        ((log_decay_hbm, log_decay_ref), (keys_hbm, keys_ref), (values_hbm, values_ref))
    ):
        loads.append(pltpu.make_async_copy(source, target, sems.at[i]))
        loads[-1].start()
    heads = log_decay_ref.shape[0]
    devices = out_ref.shape[0]
    rows = piece_rows(devices)
    per_head = HEAD_DIM // rows
    s = lax.broadcasted_iota(jnp.int32, (TILE, TILE), 0)
    until = (s <= lax.broadcasted_iota(jnp.int32, (TILE, TILE), 1)).astype(F32)
    parts = []
    total = jnp.zeros((heads, 1), F32)
    loads[0].wait()
    for j in range(BLK // TILE):
        within = dot(
            log_decay_ref[:, j * TILE:(j + 1) * TILE], until, (1, 0), lax.Precision.HIGHEST
        )
        parts.append(within + total)
        total = parts[-1][:, TILE - 1:TILE]
    cumulative = jnp.concatenate(parts, axis=1)
    ending = jnp.exp(total - cumulative)
    both = jnp.concatenate([cumulative, ending], axis=0)
    cum_ref[...] = both
    columns = both.T
    loads[1].wait()
    loads[2].wait()
    for h in range(heads):
        weighted = keys_ref[:, head_cols(h)].astype(F32) * columns[:, heads + h:heads + h + 1]
        state = dot(weighted.astype(BF16), values_ref[:, head_cols(h)], (0, 0))
        pieces = slice(h * per_head, (h + 1) * per_head)
        out_ref[pieces, :rows, :] = state.reshape(per_head, rows, HEAD_DIM)
        out_ref[pieces, rows:, :] = jnp.broadcast_to(
            total[h:h + 1].reshape(1, 1, 1), (per_head, 8, HEAD_DIM)
        )


def prefix(members_ref, out_ref, decays_ref):
    devices, rows = out_ref.shape[:2]
    decays_ref[...] = jnp.exp(members_ref[:, rows, :])
    running = jnp.zeros((rows, HEAD_DIM), F32)
    for b in range(devices):
        out_ref[b] = running
        if b < devices - 1:
            running = decays_ref[b:b + 1] * running + members_ref[b, :rows, :]


def suffix(members_ref, decays_ref, out_ref):
    devices, rows = out_ref.shape[:2]
    running = jnp.zeros((rows, HEAD_DIM), F32)
    for b in reversed(range(devices)):
        out_ref[b] = running
        if b > 0:
            running = decays_ref[b:b + 1] * running + members_ref[b]


def local_attention(queries_ref, keys_ref, values_ref, cum_ref, local_ref):
    heads = local_ref.shape[1] // HEAD_DIM
    cumulative = cum_ref[...]
    columns = cumulative.T
    for h in range(heads):
        cols = head_cols(h)
        for start in range(0, BLK, HALF):
            width = start + HALF
            scores = dot(queries_ref[start:width, cols], keys_ref[:width, cols], (1, 1))
            spread = columns[start:width, h:h + 1] - cumulative[h:h + 1, :width]
            mixing = (scores * causal_exp(spread, False)).astype(BF16)
            local_ref[start:width, cols] = dot(mixing, values_ref[:width, cols], (1, 0))


def attend(queries_ref, upstream_ref, gain_ref, cum_ref, local_ref, state_ref, att_ref, sums_ref):
    heads = state_ref.shape[0]
    columns = jnp.exp(cum_ref[...]).T
    square = jnp.zeros((BLK, HEAD_DIM), F32)
    cross = jnp.zeros((BLK, HEAD_DIM), F32)
    for h in range(heads):
        cols = head_cols(h)
        high, low = split(state_ref[h])
        carried = dot(twice(queries_ref[:, cols]), jnp.concatenate([high, low], axis=0), (1, 0))
        attended = local_ref[:, cols] + columns[:, h:h + 1] * carried
        att_ref[:, cols] = attended
        scaled = gain_ref[:, cols] * upstream_ref[:, cols].astype(F32)
        square = square + attended * attended
        cross = cross + scaled * attended
    same = eye()
    rows = []
    for summed in (square, cross):
        for j in range(BLK // TILE):
            column = jnp.sum(summed[j * TILE:(j + 1) * TILE], axis=1, keepdims=True)
            rows.append(jnp.sum(jnp.where(same, column, 0.0), axis=0, keepdims=True))
    sums = jnp.concatenate(rows, axis=0)
    for d in range(sums_ref.shape[0]):
        sums_ref[d] = sums


def grad_states(
    width, sums_ref, att_ref, upstream_ref, gain_ref, queries_ref, cum_ref, grad_ref, out_ref
):
    devices = out_ref.shape[0]
    rows = piece_rows(devices)
    per_head = HEAD_DIM // rows
    heads = devices // per_head
    sums = jnp.sum(sums_ref[...], axis=0)
    tiles = BLK // TILE
    inverse = lax.rsqrt(sums[:tiles] / width + EPSILON)
    pull = inverse * inverse * inverse * sums[tiles:] / width
    scales = jnp.concatenate([inverse, pull], axis=0).T
    columns = jnp.exp(cum_ref[...]).T
    for h in range(heads):
        cols = head_cols(h)
        for j in range(tiles):
            part = slice(j * TILE, (j + 1) * TILE)
            scaled = gain_ref[:, cols] * upstream_ref[part, cols].astype(F32)
            grad = scales[:, j:j + 1] * scaled - att_ref[part, cols] * scales[:, tiles + j:tiles + j + 1]
            grad_ref[part, cols] = grad.astype(BF16)
        weighted = queries_ref[:, cols].astype(F32) * columns[:, h:h + 1]
        state = dot(weighted.astype(BF16), grad_ref[:, cols], (0, 0))
        out_ref[h * per_head:(h + 1) * per_head] = state.reshape(per_head, rows, HEAD_DIM)


def local_grads(
    queries_ref, keys_ref, values_ref, grad_ref, cum_ref, state_ref,
    grad_queries_ref, grad_keys_ref, grad_values_ref,
):
    heads = state_ref.shape[0]
    cumulative = cum_ref[...]
    columns = cumulative.T
    for h in range(heads):
        cols = head_cols(h)
        high, low = split(state_ref[h])
        grad = grad_ref[:, cols]
        carried = dot(twice(grad), jnp.concatenate([high, low], axis=1), (1, 1))
        grad_query = jnp.exp(columns[:, h:h + 1]) * carried
        for start in range(0, BLK, HALF):
            stop = start + HALF
            query = queries_ref[start:, cols]
            key = keys_ref[start:stop, cols]
            spread = cumulative[h:h + 1, start:] - columns[start:stop, h:h + 1]
            decays = causal_exp(spread, True)
            mixing = (dot(key, query, (1, 1)) * decays).astype(BF16)
            grad_mixing = dot(values_ref[start:stop, cols], grad[start:], (1, 1)) * decays
            grad_mixing = grad_mixing.astype(BF16)
            grad_keys_ref[start:stop, cols] = dot(grad_mixing, query, (1, 0)).astype(BF16)
            grad_values_ref[start:stop, cols] = dot(mixing, grad[start:], (1, 0)).astype(BF16)
            grad_query = grad_query + dot(grad_mixing, key, (0, 0))
            grad_queries_ref[start:stop, cols] = grad_query[:HALF].astype(BF16)
            grad_query = grad_query[HALF:]


def add_carried(
    keys_ref, values_ref, cum_ref, state_ref, local_keys_ref, local_values_ref,
    grad_keys_hbm, grad_values_hbm, grad_keys_ref, grad_values_ref, sems,
):
    heads = state_ref.shape[0]
    columns = cum_ref[...].T
    stores = []
    for h in range(heads):
        cols = head_cols(h)
        high, low = split(state_ref[h])
        ending = columns[:, heads + h:heads + h + 1]
        grad_key = dot(twice(values_ref[:, cols]), jnp.concatenate([high, low], axis=1), (1, 1))
        grad_value = dot(twice(keys_ref[:, cols]), jnp.concatenate([high, low], axis=0), (1, 0))
        grad_keys_ref[:, cols] = (local_keys_ref[:, cols].astype(F32) + ending * grad_key).astype(BF16)
        grad_values_ref[:, cols] = (local_values_ref[:, cols].astype(F32) + ending * grad_value).astype(BF16)
        for i, (source, target) in enumerate(
            ((grad_keys_ref, grad_keys_hbm), (grad_values_ref, grad_values_hbm))
        ):
            stores.append(
                pltpu.make_async_copy(source.at[:, cols], target.at[:, cols], sems.at[i, h])
            )
            stores[-1].start()
    for store in stores:
        store.wait()


def call(kernel, name, out_shape, *args, flops=0, **options):
    outs = jax.tree.leaves(out_shape)
    size = sum(math.prod(a.shape) * a.dtype.itemsize for a in (*args, *outs))
    return pl.pallas_call(
        kernel,
        out_shape=out_shape,
        name=name,
        compiler_params=pltpu.CompilerParams(vmem_limit_bytes=VMEM_LIMIT),
        cost_estimate=pl.CostEstimate(flops=flops, bytes_accessed=size, transcendentals=0),
        **options,
    )(*args)


def on_device(queries, keys, values, log_decay, gain, upstream):
    tokens, columns = queries.shape
    heads = log_decay.shape[1]
    slabs = lax.axis_size("ctx")
    groups = lax.axis_size("head")
    rows = piece_rows(slabs)
    full_width = columns * groups
    gain = gain[None]
    f32 = functools.partial(jax.ShapeDtypeStruct, dtype=F32)
    bf16 = functools.partial(jax.ShapeDtypeStruct, dtype=BF16)
    square = tokens * tokens * HEAD_DIM * heads * 2
    in_hbm = pl.BlockSpec(memory_space=pltpu.HBM)
    wide = (tokens, columns)

    def exchange(x, axis):
        return lax.all_to_all(x, axis, 0, 0, tiled=True)

    def stay(x):
        return pltpu.with_memory_space_constraint(x, pltpu.HBM)

    pieces, cumulative = call(
        local_states, "local_states", (f32((slabs, rows + 8, HEAD_DIM)), f32((2 * heads, tokens))),
        stay(log_decay.T), stay(keys), stay(values), flops=square // 4,
        in_specs=[in_hbm] * 3,
        scratch_shapes=[
            pltpu.VMEM((heads, tokens), F32),
            pltpu.VMEM(wide, BF16),
            pltpu.VMEM(wide, BF16),
            pltpu.SemaphoreType.DMA((3,)),
        ],
    )
    members = exchange(pieces, "ctx")
    local = call(
        local_attention, "local_attention", f32(wide),
        queries, keys, values, cumulative, flops=2 * square,
    )
    starts, decays = call(
        prefix, "prefix", (f32((slabs, rows, HEAD_DIM)), f32((slabs, HEAD_DIM))), members
    )
    start_state = exchange(starts, "ctx").reshape(heads, HEAD_DIM, HEAD_DIM)
    attended, sums = call(
        attend, "attend", (f32(wide), f32((groups, 2 * tokens // TILE, TILE))),
        queries, upstream, gain, cumulative, local, start_state, flops=square // 2,
    )
    sums = exchange(sums, "head")
    grad_out, grad_pieces = call(
        functools.partial(grad_states, full_width), "grad_states",
        (bf16(wide), f32((slabs, rows, HEAD_DIM))),
        sums, attended, upstream, gain, queries, cumulative, flops=square // 4,
    )
    grad_members = exchange(grad_pieces, "ctx")
    grad_queries, local_keys, local_values = call(
        local_grads, "local_grads", (bf16(wide), bf16(wide), bf16(wide)),
        queries, keys, values, grad_out, cumulative, start_state, flops=5 * square,
    )
    ends = call(suffix, "suffix", f32((slabs, rows, HEAD_DIM)), grad_members, decays)
    end_state = exchange(ends, "ctx").reshape(heads, HEAD_DIM, HEAD_DIM)
    grad_keys, grad_values = call(
        add_carried, "add_carried", (bf16(wide), bf16(wide)),
        keys, values, cumulative, end_state, local_keys, local_values, flops=square,
        out_specs=[in_hbm] * 2,
        scratch_shapes=[
            pltpu.VMEM(wide, BF16),
            pltpu.VMEM(wide, BF16),
            pltpu.SemaphoreType.DMA((2, heads)),
        ],
    )
    return grad_queries, grad_keys, grad_values


def solution(mesh):
    placed = (
        P("ctx", "head"),
        P("ctx", "head"),
        P("ctx", "head"),
        P("ctx", "head"),
        P("head"),
        P("ctx", "head"),
    )
    return jax.shard_map(
        on_device,
        mesh=mesh,
        in_specs=placed,
        out_specs=(P("ctx", "head"), P("ctx", "head"), P("ctx", "head")),
        check_vma=False,
    )
```

time: 98.7 us -> 93 us (0.942)
  local copies, waits for them, and re-layouts: 12 us -> 1.07 us
  waiting for transfers between devices: 6.58 us -> 11.2 us
    unnamed x32 -> x14, local copies, waits for them, and re-layouts: 12 us -> 1.07 us
    all_to_all x2, waiting for transfers between devices: 6.58 us -> 11.2 us  [exchange(): return lax.all_to_all(x, axis, 0, 0, tiled=True)]
where the time goes in v2:
time: 93 us; the launch traced here: 92.6 us
  blocking collectives  59.2 us (64%)
  Pallas kernels  12.7 us (14%)
  waiting for transfers between devices  11.2 us (12%)
  starting transfers between devices  7.65 us (8%)
  local copies, waits for them, and re-layouts  1.07 us (1%)
    all_to_all x3, blocking collectives, exchange(): return lax.all_to_all(x, axis, 0, 0, tiled=True)  59.2 us
    pallas_call x8, Pallas kernels, call(): pl.pallas_call(kernel, out_shape=out_shape, name=name, compiler_params=pl...  12.7 us
    all_to_all x2, waiting for transfers between devices, exchange(): return lax.all_to_all(x, axis, 0, 0, tiled=True)  11.2 us
    all_to_all x2, starting transfers between devices, exchange(): return lax.all_to_all(x, axis, 0, 0, tiled=True)  7.65 us
  transfers between devices with their start and end apart: 2, of which 2 were waited for; matrix products, arithmetic and copies ran while one was open for 0% of the time, Pallas kernels for 6%

profile of v2, /device:TPU:1, one launch (start us, length us, event | category | flops | bytes accessed | tf_op | source)
XLA Modules:
  0.0 92.6 jit_solution(9453487009202647061)
XLA Ops:
  0.6 2.1 %local_states.1 = (f32[32,24,128]{2,1,0:T(8,128)S(1)}, f32[8,512]{1,0:T(8,128)S(1)}) custom-call(f32[4,512]{1,0:T(4,128)} %bitcast.9, bf16[512,512]{1,0:T(8,128)(2,1)} %keys_ref.5, bf16[512,512]{1,0:T(8,128)(2,1)} %values_ref.5), custom_call_target="tpu_custom_call" | custom-call | flops 67108864 | bytes 1466368 | tf_op jit(solution)/shard_map/local_states/pallas_call | solution.py:245
  2.7 0.0 copy-start.1
  2.7 0.0 copy-start.2
  2.8 19.9 %all_to_all.25.members_ref = f32[32,24,128]{2,1,0:T(8,128)S(1)} all-to-all(f32[32,24,128]{2,1,0:T(8,128)S(1)} %get-tuple-element.17), channel_id=1, replica_groups=mesh['ctx'=32,'head'=16] {'ctx'}, dimensions={0} | all-to-all | bytes 786432 | tf_op jit(solution)/shard_map/all_to_all | solution.py:270
  22.7 0.0 copy-start
  22.7 0.8 prefix.1
  23.5 3.9 %all-to-all-start.1 = ((f32[32,16,128]{2,1,0:T(8,128)}), f32[32,16,128]{2,1,0:T(8,128)S(1)}, u32[]{:S(2)}, u32[]{:S(2)}) async-start(f32[32,16,128]{2,1,0:T(8,128)} %get-tuple-element.18), calls=%async_computation.1 | async-start | bytes 524288 | tf_op jit(solution)/shard_map/all_to_all | solution.py:270
  27.4 0.0 copy-done.1
  27.4 0.0 copy-done.2
  27.4 0.0 copy-done
  27.4 0.0 copy-start.3
  27.4 1.6 %local_attention.1.local_ref = f32[512,512]{1,0:T(8,128)S(1)} custom-call(bf16[512,512]{1,0:T(8,128)(2,1)S(1)} %copy-done, bf16[512,512]{1,0:T(8,128)(2,1)S(1)} %copy-done.1, bf16[512,512]{1,0:T(8,128)(2,1)S(1)} %copy-done.2, f32[8,512]{1,0:T(8,128)S(1)} %get-tuple-element.16.cum_ref), custom_call_target="tpu_custom_call" | custom-call | flops 536870912 | bytes 2637824 | tf_op jit(solution)/shard_map/local_attention/pallas_call | solution.py:245
  29.1 0.0 copy-start.4
  29.1 7.3 %all-to-all-done.1 = f32[32,16,128]{2,1,0:T(8,128)S(1)} async-done(((f32[32,16,128]{2,1,0:T(8,128)}), f32[32,16,128]{2,1,0:T(8,128)S(1)}, u32[]{:S(2)}, u32[]{:S(2)}) %all-to-all-start.1) | async-done | bytes 262176 | tf_op jit(solution)/shard_map/all_to_all | solution.py:270
  36.4 0.0 copy-done.3
  36.4 0.0 copy-done.4
  36.4 0.7 attend.1
  37.1 25.1 %all_to_all.26.sums_ref = f32[16,8,128]{2,1,0:T(8,128)S(1)} all-to-all(f32[16,8,128]{2,1,0:T(8,128)S(1)} %get-tuple-element.19), channel_id=1, replica_groups=mesh['ctx'=32,'head'=16] {'head'}, dimensions={0} | all-to-all | bytes 131072 | tf_op jit(solution)/shard_map/all_to_all | solution.py:270
  62.2 1.1 %grad_states.1 = (bf16[512,512]{1,0:T(8,128)(2,1)S(1)}, f32[32,16,128]{2,1,0:T(8,128)S(1)}) custom-call(f32[16,8,128]{2,1,0:T(8,128)S(1)} %all_to_all.26.sums_ref, f32[512,512]{1,0:T(8,128)S(1)} %get-tuple-element.20.att_ref, bf16[512,512]{1,0:T(8,128)(2,1)S(1)} %copy-done.3, f32[1,512]{1,0:T(1,128)S(1)} %bitcast.8, bf16[512,512]{1,0:T(8,128)(2,1)S(1)} %copy-done, ...), custom_call_target="tpu_custom_call" | custom-call | flops 67108864 | bytes 2967552 | tf_op jit(solution)/shard_map/grad_states/pallas_call | solution.py:245
  63.3 0.0 copy-start.5
  63.3 14.2 %all_to_all.27.members_ref = f32[32,16,128]{2,1,0:T(8,128)S(1)} all-to-all(f32[32,16,128]{2,1,0:T(8,128)S(1)} %get-tuple-element.23), channel_id=1, replica_groups=mesh['ctx'=32,'head'=16] {'ctx'}, dimensions={0} | all-to-all | bytes 524288 | tf_op jit(solution)/shard_map/all_to_all | solution.py:270
  77.5 0.8 suffix.1
  78.3 0.0 copy-done.5
  78.3 3.8 %all-to-all-start.4 = ((f32[32,16,128]{2,1,0:T(8,128)}), f32[32,16,128]{2,1,0:T(8,128)S(1)}, u32[]{:S(2)}, u32[]{:S(2)}) async-start(f32[32,16,128]{2,1,0:T(8,128)} %suffix.1), calls=%async_computation.4 | async-start | bytes 524288 | tf_op jit(solution)/shard_map/all_to_all | solution.py:270
  82.1 0.0 copy-start.6
  82.1 1.0 %copy-done.6 = bf16[512,512]{1,0:T(8,128)(2,1)S(1)} copy-done((bf16[512,512]{1,0:T(8,128)(2,1)S(1)}, bf16[512,512]{1,0:T(8,128)(2,1)}, u32[]{:S(2)}) %copy-start.6) | copy-done | bytes 524312
  83.1 4.1 %local_grads.1 = (bf16[512,512]{1,0:T(8,128)(2,1)}, bf16[512,512]{1,0:T(8,128)(2,1)S(1)}, bf16[512,512]{1,0:T(8,128)(2,1)S(1)}) custom-call(bf16[512,512]{1,0:T(8,128)(2,1)S(1)} %copy-done, bf16[512,512]{1,0:T(8,128)(2,1)S(1)} %copy-done.1, bf16[512,512]{1,0:T(8,128)(2,1)S(1)} %copy-done.2, bf16[512,512]{1,0:T(8,128)(2,1)S(1)} %copy-done.6, ...), custom_call_target="tpu_custom_call" | custom-call | flops 1342177280 | bytes 3948544 | tf_op jit(solution)/shard_map/local_grads/pallas_call | solution.py:245
  87.2 3.9 %all-to-all-done.4 = f32[32,16,128]{2,1,0:T(8,128)S(1)} async-done(((f32[32,16,128]{2,1,0:T(8,128)}), f32[32,16,128]{2,1,0:T(8,128)S(1)}, u32[]{:S(2)}, u32[]{:S(2)}) %all-to-all-start.4) | async-done | bytes 262176 | tf_op jit(solution)/shard_map/all_to_all | solution.py:270
  91.1 1.5 %add_carried.1 = (bf16[512,512]{1,0:T(8,128)(2,1)}, bf16[512,512]{1,0:T(8,128)(2,1)}) custom-call(bf16[512,512]{1,0:T(8,128)(2,1)S(1)} %copy-done.1, bf16[512,512]{1,0:T(8,128)(2,1)S(1)} %copy-done.2, f32[8,512]{1,0:T(8,128)S(1)} %get-tuple-element.16.cum_ref, f32[4,128,128]{2,1,0:T(8,128)S(1)} %bitcast.4, ...), custom_call_target="tpu_custom_call" | custom-call | flops 268435456 | bytes 3424256 | tf_op jit(solution)/shard_map/add_carried/pallas_call | solution.py:245
Async XLA Ops:
  2.7 24.7 %copy-start.1 = (bf16[512,512]{1,0:T(8,128)(2,1)S(1)}, bf16[512,512]{1,0:T(8,128)(2,1)}, u32[]{:S(2)}) copy-start(bf16[512,512]{1,0:T(8,128)(2,1)} %keys_ref.5) | copy-start | bytes 1572868
  2.7 24.6 %copy-start.2 = (bf16[512,512]{1,0:T(8,128)(2,1)S(1)}, bf16[512,512]{1,0:T(8,128)(2,1)}, u32[]{:S(2)}) copy-start(bf16[512,512]{1,0:T(8,128)(2,1)} %values_ref.5) | copy-start | bytes 1572868
  22.7 4.7 %copy-start = (bf16[512,512]{1,0:T(8,128)(2,1)S(1)}, bf16[512,512]{1,0:T(8,128)(2,1)}, u32[]{:S(2)}) copy-start(bf16[512,512]{1,0:T(8,128)(2,1)} %queries_ref.7) | copy-start | bytes 1572868
  23.5 12.9 %all-to-all-start.1 = ((f32[32,16,128]{2,1,0:T(8,128)}), f32[32,16,128]{2,1,0:T(8,128)S(1)}, u32[]{:S(2)}, u32[]{:S(2)}) async-start(f32[32,16,128]{2,1,0:T(8,128)} %get-tuple-element.18), calls=%async_computation.1 | async-start | bytes 524288 | tf_op jit(solution)/shard_map/all_to_all | solution.py:270
  27.4 9.0 %copy-start.3 = (bf16[512,512]{1,0:T(8,128)(2,1)S(1)}, bf16[512,512]{1,0:T(8,128)(2,1)}, u32[]{:S(2)}) copy-start(bf16[512,512]{1,0:T(8,128)(2,1)} %upstream_ref.3) | copy-start | bytes 1572868
  29.1 7.3 %copy-start.4 = (f32[512]{0:T(512)S(1)}, f32[512]{0:T(512)}, u32[]{:S(2)}) copy-start(f32[512]{0:T(512)} %param.10) | copy-start | bytes 6148
  63.3 15.0 %copy-start.5 = (bf16[512,512]{1,0:T(8,128)(2,1)}, bf16[512,512]{1,0:T(8,128)(2,1)S(1)}, u32[]{:S(2)}) copy-start(bf16[512,512]{1,0:T(8,128)(2,1)S(1)} %get-tuple-element.21.grad_ref) | copy-start | bytes 1572868
  78.3 12.8 %all-to-all-start.4 = ((f32[32,16,128]{2,1,0:T(8,128)}), f32[32,16,128]{2,1,0:T(8,128)S(1)}, u32[]{:S(2)}, u32[]{:S(2)}) async-start(f32[32,16,128]{2,1,0:T(8,128)} %suffix.1), calls=%async_computation.4 | async-start | bytes 524288 | tf_op jit(solution)/shard_map/all_to_all | solution.py:270
  82.1 1.0 %copy-start.6 = (bf16[512,512]{1,0:T(8,128)(2,1)S(1)}, bf16[512,512]{1,0:T(8,128)(2,1)}, u32[]{:S(2)}) copy-start(bf16[512,512]{1,0:T(8,128)(2,1)} %copy-done.5) | copy-start | bytes 1572868

commit v3 on v2

--- a/solution.py
+++ b/solution.py
@@ -95,29 +95,35 @@
         weighted = keys_ref[:, head_cols(h)].astype(F32) * columns[:, heads + h:heads + h + 1]
         state = dot(weighted.astype(BF16), values_ref[:, head_cols(h)], (0, 0))
         pieces = slice(h * per_head, (h + 1) * per_head)
-        out_ref[pieces, :rows, :] = state.reshape(per_head, rows, HEAD_DIM)
-        out_ref[pieces, rows:, :] = jnp.broadcast_to(
-            total[h:h + 1].reshape(1, 1, 1), (per_head, 8, HEAD_DIM)
-        )
+        out_ref[pieces, :rows, 0, :] = state.reshape(per_head, rows, HEAD_DIM)
+        out_ref[pieces, rows, 0, :] = jnp.broadcast_to(total[h:h + 1], (per_head, HEAD_DIM))
+
+
+def rotated(size):
+    return [(size * 5 // 8 + i) % size for i in range(size)]
 
 
 def prefix(members_ref, out_ref, decays_ref):
     devices, rows = out_ref.shape[:2]
-    decays_ref[...] = jnp.exp(members_ref[:, rows, :])
+    order = rotated(devices)
+    decays_ref[...] = jnp.exp(members_ref[:, rows, 0, :])
     running = jnp.zeros((rows, HEAD_DIM), F32)
     for b in range(devices):
-        out_ref[b] = running
+        i = order.index(b)
+        out_ref[i] = running
         if b < devices - 1:
-            running = decays_ref[b:b + 1] * running + members_ref[b, :rows, :]
+            running = decays_ref[i:i + 1] * running + members_ref[i, :rows, 0, :]
 
 
 def suffix(members_ref, decays_ref, out_ref):
     devices, rows = out_ref.shape[:2]
+    order = rotated(devices)
     running = jnp.zeros((rows, HEAD_DIM), F32)
     for b in reversed(range(devices)):
-        out_ref[b] = running
+        i = order.index(b)
+        out_ref[i] = running
         if b > 0:
-            running = decays_ref[b:b + 1] * running + members_ref[b]
+            running = decays_ref[i:i + 1] * running + members_ref[i]
 
 
 def local_attention(queries_ref, keys_ref, values_ref, cum_ref, local_ref):
@@ -267,13 +273,14 @@
     wide = (tokens, columns)
 
     def exchange(x, axis):
-        return lax.all_to_all(x, axis, 0, 0, tiled=True)
+        order = rotated(lax.axis_size(axis))
+        return lax.all_to_all(x, axis, 0, 0, tiled=True, axis_index_groups=[order])
 
     def stay(x):
         return pltpu.with_memory_space_constraint(x, pltpu.HBM)
 
     pieces, cumulative = call(
-        local_states, "local_states", (f32((slabs, rows + 8, HEAD_DIM)), f32((2 * heads, tokens))),
+        local_states, "local_states", (f32((slabs, rows + 1, 1, HEAD_DIM)), f32((2 * heads, tokens))),
         stay(log_decay.T), stay(keys), stay(values), flops=square // 4,
         in_specs=[in_hbm] * 3,
         scratch_shapes=[

time: 93 us -> 83.1 us (0.89)
  blocking collectives: 59.2 us -> 49.2 us
  waiting for transfers between devices: 11.2 us -> 2.43 us
  starting transfers between devices: 7.65 us -> 16.3 us
    all_to_all x3, blocking collectives: 59.2 us -> 49.2 us  [exchange(): return lax.all_to_all(x, axis, 0, 0, tiled=True, axis_index_groups=[order])]
    all_to_all x2, waiting for transfers between devices: 11.2 us -> 2.43 us  [exchange(): return lax.all_to_all(x, axis, 0, 0, tiled=True, axis_index_groups=[order])]
    all_to_all x2, starting transfers between devices: 7.65 us -> 16.3 us  [exchange(): return lax.all_to_all(x, axis, 0, 0, tiled=True, axis_index_groups=[order])]
  transfers between devices with their start and end apart: 2 -> 2, of which waited for: 2 -> 1; matrix products, arithmetic and copies ran while one was open for 0% -> 0% of each run, Pallas kernels for 6% -> 7%
where the time goes in v3:
time: 83.1 us; the launch traced here: 82.6 us
  blocking collectives  49.2 us (59%)
  starting transfers between devices  16.3 us (20%)
  Pallas kernels  12.9 us (16%)
  waiting for transfers between devices  2.43 us (3%)
  local copies, waits for them, and re-layouts  1.07 us (1%)
    all_to_all x3, blocking collectives, exchange(): return lax.all_to_all(x, axis, 0, 0, tiled=True, axis_index_groups=[order])  49.2 us
    all_to_all x2, starting transfers between devices, exchange(): return lax.all_to_all(x, axis, 0, 0, tiled=True, axis_index_groups=[order])  16.3 us
    pallas_call x8, Pallas kernels, call(): pl.pallas_call(kernel, out_shape=out_shape, name=name, compiler_params=pl...  12.9 us
    all_to_all x2, waiting for transfers between devices, exchange(): return lax.all_to_all(x, axis, 0, 0, tiled=True, axis_index_groups=[order])  2.43 us
  transfers between devices with their start and end apart: 2, of which 1 were waited for; matrix products, arithmetic and copies ran while one was open for 0% of the time, Pallas kernels for 7%

profile of v3, /device:TPU:1, one launch (start us, length us, event | category | flops | bytes accessed | tf_op | source)
XLA Modules:
  0.0 82.6 jit_solution(1364443650166188886)
XLA Ops:
  0.6 0.0 copy-start.2
  0.6 2.2 %local_states.1 = (f32[32,17,1,128]{3,2,1,0:T(1,128)S(1)}, f32[8,512]{1,0:T(8,128)S(1)}) custom-call(f32[4,512]{1,0:T(4,128)} %bitcast.9, bf16[512,512]{1,0:T(8,128)(2,1)} %keys_ref.5, bf16[512,512]{1,0:T(8,128)(2,1)} %values_ref.5), custom_call_target="tpu_custom_call" | custom-call | flops 67108864 | bytes 1351680 | tf_op jit(solution)/shard_map/local_states/pallas_call | solution.py:251
  2.8 0.0 copy-start.1
  2.8 18.1 %all_to_all.25.members_ref = f32[32,17,1,128]{3,2,1,0:T(1,128)S(1)} all-to-all(f32[32,17,1,128]{3,2,1,0:T(1,128)S(1)} %get-tuple-element.17), channel_id=1, replica_groups={{320,336,352,368,384,400,416,432,448,464,480,496,0,16,32,48,64,80,96,11..., dimensions={0} | all-to-all | bytes 557056 | tf_op jit(solution)/shard_map/all_to_all | solution.py:277
  20.9 0.0 copy-start
  21.0 0.9 %prefix.1 = (f32[32,16,128]{2,1,0:T(8,128)}, f32[32,128]{1,0:T(8,128)S(1)}) custom-call(f32[32,17,1,128]{3,2,1,0:T(1,128)S(1)} %all_to_all.25.members_ref), custom_call_target="tpu_custom_call" | custom-call | bytes 557056 | tf_op jit(solution)/shard_map/prefix/pallas_call | solution.py:251
  21.8 8.1 %all-to-all-start.1 = ((f32[32,16,128]{2,1,0:T(8,128)}), f32[32,16,128]{2,1,0:T(8,128)S(1)}, u32[]{:S(2)}, u32[]{:S(2)}) async-start(f32[32,16,128]{2,1,0:T(8,128)} %get-tuple-element.18), calls=%async_computation.1 | async-start | bytes 524288 | tf_op jit(solution)/shard_map/all_to_all | solution.py:277
  29.9 0.0 copy-done.2
  29.9 0.0 copy-done.1
  29.9 0.0 copy-done
  30.0 0.0 copy-start.3
  30.0 1.6 %local_attention.1.local_ref = f32[512,512]{1,0:T(8,128)S(1)} custom-call(bf16[512,512]{1,0:T(8,128)(2,1)S(1)} %copy-done, bf16[512,512]{1,0:T(8,128)(2,1)S(1)} %copy-done.1, bf16[512,512]{1,0:T(8,128)(2,1)S(1)} %copy-done.2, f32[8,512]{1,0:T(8,128)S(1)} %get-tuple-element.16.cum_ref), custom_call_target="tpu_custom_call" | custom-call | flops 536870912 | bytes 2637824 | tf_op jit(solution)/shard_map/local_attention/pallas_call | solution.py:251
  31.6 0.0 copy-start.4
  31.6 2.4 %all-to-all-done.1 = f32[32,16,128]{2,1,0:T(8,128)S(1)} async-done(((f32[32,16,128]{2,1,0:T(8,128)}), f32[32,16,128]{2,1,0:T(8,128)S(1)}, u32[]{:S(2)}, u32[]{:S(2)}) %all-to-all-start.1) | async-done | bytes 262176 | tf_op jit(solution)/shard_map/all_to_all | solution.py:277
  34.1 0.0 copy-done.3
  34.1 0.0 copy-done.4
  34.1 0.7 attend.1
  34.8 17.9 %all_to_all.26.sums_ref = f32[16,8,128]{2,1,0:T(8,128)S(1)} all-to-all(f32[16,8,128]{2,1,0:T(8,128)S(1)} %get-tuple-element.19), channel_id=1, replica_groups={{10,11,12,13,14,15,0,1,2,3,4,5,6,7,8,9},{26,27,28,29,30,31,16,17,18,19,..., dimensions={0} | all-to-all | bytes 131072 | tf_op jit(solution)/shard_map/all_to_all | solution.py:277
  52.7 1.1 %grad_states.1 = (bf16[512,512]{1,0:T(8,128)(2,1)S(1)}, f32[32,16,128]{2,1,0:T(8,128)S(1)}) custom-call(f32[16,8,128]{2,1,0:T(8,128)S(1)} %all_to_all.26.sums_ref, f32[512,512]{1,0:T(8,128)S(1)} %get-tuple-element.20.att_ref, bf16[512,512]{1,0:T(8,128)(2,1)S(1)} %copy-done.3, f32[1,512]{1,0:T(1,128)S(1)} %bitcast.8, bf16[512,512]{1,0:T(8,128)(2,1)S(1)} %copy-done, ...), custom_call_target="tpu_custom_call" | custom-call | flops 67108864 | bytes 2967552 | tf_op jit(solution)/shard_map/grad_states/pallas_call | solution.py:251
  53.8 0.0 copy-start.5
  53.8 13.2 %all_to_all.27.members_ref = f32[32,16,128]{2,1,0:T(8,128)S(1)} all-to-all(f32[32,16,128]{2,1,0:T(8,128)S(1)} %get-tuple-element.23), channel_id=1, replica_groups={{320,336,352,368,384,400,416,432,448,464,480,496,0,16,32,48,64,80,96,11..., dimensions={0} | all-to-all | bytes 524288 | tf_op jit(solution)/shard_map/all_to_all | solution.py:277
  67.0 0.8 suffix.1
  67.7 0.0 copy-done.5
  67.8 8.2 %all-to-all-start.4 = ((f32[32,16,128]{2,1,0:T(8,128)}), f32[32,16,128]{2,1,0:T(8,128)S(1)}, u32[]{:S(2)}, u32[]{:S(2)}) async-start(f32[32,16,128]{2,1,0:T(8,128)} %suffix.1), calls=%async_computation.4 | async-start | bytes 524288 | tf_op jit(solution)/shard_map/all_to_all | solution.py:277
  76.0 0.0 copy-start.6
  76.0 1.0 %copy-done.6 = bf16[512,512]{1,0:T(8,128)(2,1)S(1)} copy-done((bf16[512,512]{1,0:T(8,128)(2,1)S(1)}, bf16[512,512]{1,0:T(8,128)(2,1)}, u32[]{:S(2)}) %copy-start.6) | copy-done | bytes 524312
  77.0 4.1 %local_grads.1 = (bf16[512,512]{1,0:T(8,128)(2,1)}, bf16[512,512]{1,0:T(8,128)(2,1)S(1)}, bf16[512,512]{1,0:T(8,128)(2,1)S(1)}) custom-call(bf16[512,512]{1,0:T(8,128)(2,1)S(1)} %copy-done, bf16[512,512]{1,0:T(8,128)(2,1)S(1)} %copy-done.1, bf16[512,512]{1,0:T(8,128)(2,1)S(1)} %copy-done.2, bf16[512,512]{1,0:T(8,128)(2,1)S(1)} %copy-done.6, ...), custom_call_target="tpu_custom_call" | custom-call | flops 1342177280 | bytes 3948544 | tf_op jit(solution)/shard_map/local_grads/pallas_call | solution.py:251
  81.1 0.0 all-to-all-done.4
  81.1 1.5 %add_carried.1 = (bf16[512,512]{1,0:T(8,128)(2,1)}, bf16[512,512]{1,0:T(8,128)(2,1)}) custom-call(bf16[512,512]{1,0:T(8,128)(2,1)S(1)} %copy-done.1, bf16[512,512]{1,0:T(8,128)(2,1)S(1)} %copy-done.2, f32[8,512]{1,0:T(8,128)S(1)} %get-tuple-element.16.cum_ref, f32[4,128,128]{2,1,0:T(8,128)S(1)} %bitcast.4, ...), custom_call_target="tpu_custom_call" | custom-call | flops 268435456 | bytes 3424256 | tf_op jit(solution)/shard_map/add_carried/pallas_call | solution.py:251
Async XLA Ops:
  0.6 29.3 %copy-start.2 = (bf16[512,512]{1,0:T(8,128)(2,1)S(1)}, bf16[512,512]{1,0:T(8,128)(2,1)}, u32[]{:S(2)}) copy-start(bf16[512,512]{1,0:T(8,128)(2,1)} %values_ref.5) | copy-start | bytes 1572868
  2.8 27.1 %copy-start.1 = (bf16[512,512]{1,0:T(8,128)(2,1)S(1)}, bf16[512,512]{1,0:T(8,128)(2,1)}, u32[]{:S(2)}) copy-start(bf16[512,512]{1,0:T(8,128)(2,1)} %keys_ref.5) | copy-start | bytes 1572868
  20.9 9.0 %copy-start = (bf16[512,512]{1,0:T(8,128)(2,1)S(1)}, bf16[512,512]{1,0:T(8,128)(2,1)}, u32[]{:S(2)}) copy-start(bf16[512,512]{1,0:T(8,128)(2,1)} %queries_ref.7) | copy-start | bytes 1572868
  21.8 12.3 %all-to-all-start.1 = ((f32[32,16,128]{2,1,0:T(8,128)}), f32[32,16,128]{2,1,0:T(8,128)S(1)}, u32[]{:S(2)}, u32[]{:S(2)}) async-start(f32[32,16,128]{2,1,0:T(8,128)} %get-tuple-element.18), calls=%async_computation.1 | async-start | bytes 524288 | tf_op jit(solution)/shard_map/all_to_all | solution.py:277
  30.0 4.1 %copy-start.3 = (bf16[512,512]{1,0:T(8,128)(2,1)S(1)}, bf16[512,512]{1,0:T(8,128)(2,1)}, u32[]{:S(2)}) copy-start(bf16[512,512]{1,0:T(8,128)(2,1)} %upstream_ref.3) | copy-start | bytes 1572868
  31.6 2.4 %copy-start.4 = (f32[512]{0:T(512)S(1)}, f32[512]{0:T(512)}, u32[]{:S(2)}) copy-start(f32[512]{0:T(512)} %param.10) | copy-start | bytes 6148
  53.8 14.0 %copy-start.5 = (bf16[512,512]{1,0:T(8,128)(2,1)}, bf16[512,512]{1,0:T(8,128)(2,1)S(1)}, u32[]{:S(2)}) copy-start(bf16[512,512]{1,0:T(8,128)(2,1)S(1)} %get-tuple-element.21.grad_ref) | copy-start | bytes 1572868
  67.8 13.4 %all-to-all-start.4 = ((f32[32,16,128]{2,1,0:T(8,128)}), f32[32,16,128]{2,1,0:T(8,128)S(1)}, u32[]{:S(2)}, u32[]{:S(2)}) async-start(f32[32,16,128]{2,1,0:T(8,128)} %suffix.1), calls=%async_computation.4 | async-start | bytes 524288 | tf_op jit(solution)/shard_map/all_to_all | solution.py:277
  76.0 1.0 %copy-start.6 = (bf16[512,512]{1,0:T(8,128)(2,1)S(1)}, bf16[512,512]{1,0:T(8,128)(2,1)}, u32[]{:S(2)}) copy-start(bf16[512,512]{1,0:T(8,128)(2,1)} %copy-done.5) | copy-start | bytes 1572868

commit v4 on v3

--- a/solution.py
+++ b/solution.py
@@ -43,17 +43,17 @@
     return rows == lax.broadcasted_iota(jnp.int32, (TILE, TILE), 1)
 
 
-def causal_exp(spread, later):
+def decay_tile(cumulative, columns, h, start):
+    stop = start + HALF
+    spread = columns[start:stop, h:h + 1] - cumulative[h:h + 1, :stop]
     rows = lax.broadcasted_iota(jnp.int32, (HALF, HALF), 0)
-    columns = lax.broadcasted_iota(jnp.int32, (HALF, HALF), 1)
-    width = spread.shape[1]
-    if later:
-        diagonal = jnp.where(columns >= rows, spread[:, :HALF], -1e30)
-        parts = [diagonal] + [spread[:, HALF:]] * (width > HALF)
-    else:
-        diagonal = jnp.where(columns <= rows, spread[:, width - HALF:], -1e30)
-        parts = [spread[:, :width - HALF]] * (width > HALF) + [diagonal]
+    causal = lax.broadcasted_iota(jnp.int32, (HALF, HALF), 1) <= rows
+    parts = [spread[:, :start]] * (start > 0) + [jnp.where(causal, spread[:, start:], -1e30)]
     return jnp.concatenate([jnp.exp(part) for part in parts], axis=1)
+
+
+def add_halves(first, second):
+    return jnp.concatenate([second[:, :HALF] + first, second[:, HALF:]], axis=1)
 
 
 def piece_rows(devices):
@@ -135,8 +135,7 @@
         for start in range(0, BLK, HALF):
             width = start + HALF
             scores = dot(queries_ref[start:width, cols], keys_ref[:width, cols], (1, 1))
-            spread = columns[start:width, h:h + 1] - cumulative[h:h + 1, :width]
-            mixing = (scores * causal_exp(spread, False)).astype(BF16)
+            mixing = (scores * decay_tile(cumulative, columns, h, start)).astype(BF16)
             local_ref[start:width, cols] = dot(mixing, values_ref[:width, cols], (1, 0))
 
 
@@ -200,23 +199,22 @@
     for h in range(heads):
         cols = head_cols(h)
         high, low = split(state_ref[h])
-        grad = grad_ref[:, cols]
-        carried = dot(twice(grad), jnp.concatenate([high, low], axis=1), (1, 1))
-        grad_query = jnp.exp(columns[:, h:h + 1]) * carried
+        both = jnp.concatenate([high, low], axis=1)
+        key_sums, value_sums = [], []
         for start in range(0, BLK, HALF):
             stop = start + HALF
-            query = queries_ref[start:, cols]
-            key = keys_ref[start:stop, cols]
-            spread = cumulative[h:h + 1, start:] - columns[start:stop, h:h + 1]
-            decays = causal_exp(spread, True)
-            mixing = (dot(key, query, (1, 1)) * decays).astype(BF16)
-            grad_mixing = dot(values_ref[start:stop, cols], grad[start:], (1, 1)) * decays
-            grad_mixing = grad_mixing.astype(BF16)
-            grad_keys_ref[start:stop, cols] = dot(grad_mixing, query, (1, 0)).astype(BF16)
-            grad_values_ref[start:stop, cols] = dot(mixing, grad[start:], (1, 0)).astype(BF16)
-            grad_query = grad_query + dot(grad_mixing, key, (0, 0))
-            grad_queries_ref[start:stop, cols] = grad_query[:HALF].astype(BF16)
-            grad_query = grad_query[HALF:]
+            grad = grad_ref[start:stop, cols]
+            query = queries_ref[start:stop, cols]
+            decays = decay_tile(cumulative, columns, h, start)
+            mixing = (dot(query, keys_ref[:stop, cols], (1, 1)) * decays).astype(BF16)
+            grad_mixing = (dot(grad, values_ref[:stop, cols], (1, 1)) * decays).astype(BF16)
+            carried = jnp.exp(columns[start:stop, h:h + 1]) * dot(twice(grad), both, (1, 1))
+            grad_query = carried + dot(grad_mixing, keys_ref[:stop, cols], (1, 0))
+            grad_queries_ref[start:stop, cols] = grad_query.astype(BF16)
+            key_sums.append(dot(query, grad_mixing, (0, 0)))
+            value_sums.append(dot(grad, mixing, (0, 0)))
+        grad_keys_ref[:, cols] = add_halves(*key_sums).T.astype(BF16)
+        grad_values_ref[:, cols] = add_halves(*value_sums).T.astype(BF16)
 
 
 def add_carried(

time: 83.1 us -> 82.3 us (level)
  transfers between devices with their start and end apart: 2 -> 2, of which waited for: 1 -> 1; matrix products, arithmetic and copies ran while one was open for 0% -> 0% of each run, Pallas kernels for 7% -> 6%
where the time goes in v4:
time: 82.3 us; the launch traced here: 81.9 us
  blocking collectives  49.2 us (60%)
  starting transfers between devices  16.3 us (20%)
  Pallas kernels  12.1 us (15%)
  waiting for transfers between devices  2.43 us (3%)
  local copies, waits for them, and re-layouts  1.07 us (1%)
    all_to_all x3, blocking collectives, exchange(): return lax.all_to_all(x, axis, 0, 0, tiled=True, axis_index_groups=[order])  49.2 us
    all_to_all x2, starting transfers between devices, exchange(): return lax.all_to_all(x, axis, 0, 0, tiled=True, axis_index_groups=[order])  16.3 us
    pallas_call x8, Pallas kernels, call(): pl.pallas_call(kernel, out_shape=out_shape, name=name, compiler_params=pl...  12.1 us
    all_to_all x2, waiting for transfers between devices, exchange(): return lax.all_to_all(x, axis, 0, 0, tiled=True, axis_index_groups=[order])  2.43 us
  transfers between devices with their start and end apart: 2, of which 1 were waited for; matrix products, arithmetic and copies ran while one was open for 0% of the time, Pallas kernels for 6%

profile of v4, /device:TPU:1, one launch (start us, length us, event | category | flops | bytes accessed | tf_op | source)
XLA Modules:
  0.0 81.9 jit_solution(8375402145826766116)
XLA Ops:
  0.6 0.0 copy-start.2
  0.6 2.2 %local_states.1 = (f32[32,17,1,128]{3,2,1,0:T(1,128)S(1)}, f32[8,512]{1,0:T(8,128)S(1)}) custom-call(f32[4,512]{1,0:T(4,128)} %bitcast.9, bf16[512,512]{1,0:T(8,128)(2,1)} %keys_ref.5, bf16[512,512]{1,0:T(8,128)(2,1)} %values_ref.5), custom_call_target="tpu_custom_call" | custom-call | flops 67108864 | bytes 1351680 | tf_op jit(solution)/shard_map/local_states/pallas_call | solution.py:249
  2.8 0.0 copy-start.1
  2.8 18.1 %all_to_all.25.members_ref = f32[32,17,1,128]{3,2,1,0:T(1,128)S(1)} all-to-all(f32[32,17,1,128]{3,2,1,0:T(1,128)S(1)} %get-tuple-element.17), channel_id=1, replica_groups={{320,336,352,368,384,400,416,432,448,464,480,496,0,16,32,48,64,80,96,11..., dimensions={0} | all-to-all | bytes 557056 | tf_op jit(solution)/shard_map/all_to_all | solution.py:275
  20.9 0.0 copy-start
  21.0 0.9 %prefix.1 = (f32[32,16,128]{2,1,0:T(8,128)}, f32[32,128]{1,0:T(8,128)S(1)}) custom-call(f32[32,17,1,128]{3,2,1,0:T(1,128)S(1)} %all_to_all.25.members_ref), custom_call_target="tpu_custom_call" | custom-call | bytes 557056 | tf_op jit(solution)/shard_map/prefix/pallas_call | solution.py:249
  21.8 8.1 %all-to-all-start.1 = ((f32[32,16,128]{2,1,0:T(8,128)}), f32[32,16,128]{2,1,0:T(8,128)S(1)}, u32[]{:S(2)}, u32[]{:S(2)}) async-start(f32[32,16,128]{2,1,0:T(8,128)} %get-tuple-element.18), calls=%async_computation.1 | async-start | bytes 524288 | tf_op jit(solution)/shard_map/all_to_all | solution.py:275
  29.9 0.0 copy-done.2
  29.9 0.0 copy-done.1
  29.9 0.0 copy-done
  30.0 0.0 copy-start.3
  30.0 1.6 %local_attention.1.local_ref = f32[512,512]{1,0:T(8,128)S(1)} custom-call(bf16[512,512]{1,0:T(8,128)(2,1)S(1)} %copy-done, bf16[512,512]{1,0:T(8,128)(2,1)S(1)} %copy-done.1, bf16[512,512]{1,0:T(8,128)(2,1)S(1)} %copy-done.2, f32[8,512]{1,0:T(8,128)S(1)} %get-tuple-element.16.cum_ref), custom_call_target="tpu_custom_call" | custom-call | flops 536870912 | bytes 2637824 | tf_op jit(solution)/shard_map/local_attention/pallas_call | solution.py:249
  31.6 0.0 copy-start.4
  31.6 2.4 %all-to-all-done.1 = f32[32,16,128]{2,1,0:T(8,128)S(1)} async-done(((f32[32,16,128]{2,1,0:T(8,128)}), f32[32,16,128]{2,1,0:T(8,128)S(1)}, u32[]{:S(2)}, u32[]{:S(2)}) %all-to-all-start.1) | async-done | bytes 262176 | tf_op jit(solution)/shard_map/all_to_all | solution.py:275
  34.1 0.0 copy-done.3
  34.1 0.0 copy-done.4
  34.1 0.7 attend.1
  34.8 17.9 %all_to_all.26.sums_ref = f32[16,8,128]{2,1,0:T(8,128)S(1)} all-to-all(f32[16,8,128]{2,1,0:T(8,128)S(1)} %get-tuple-element.19), channel_id=1, replica_groups={{10,11,12,13,14,15,0,1,2,3,4,5,6,7,8,9},{26,27,28,29,30,31,16,17,18,19,..., dimensions={0} | all-to-all | bytes 131072 | tf_op jit(solution)/shard_map/all_to_all | solution.py:275
  52.7 1.1 %grad_states.1 = (bf16[512,512]{1,0:T(8,128)(2,1)S(1)}, f32[32,16,128]{2,1,0:T(8,128)S(1)}) custom-call(f32[16,8,128]{2,1,0:T(8,128)S(1)} %all_to_all.26.sums_ref, f32[512,512]{1,0:T(8,128)S(1)} %get-tuple-element.20.att_ref, bf16[512,512]{1,0:T(8,128)(2,1)S(1)} %copy-done.3, f32[1,512]{1,0:T(1,128)S(1)} %bitcast.8, bf16[512,512]{1,0:T(8,128)(2,1)S(1)} %copy-done, ...), custom_call_target="tpu_custom_call" | custom-call | flops 67108864 | bytes 2967552 | tf_op jit(solution)/shard_map/grad_states/pallas_call | solution.py:249
  53.8 0.0 copy-start.5
  53.8 13.2 %all_to_all.27.members_ref = f32[32,16,128]{2,1,0:T(8,128)S(1)} all-to-all(f32[32,16,128]{2,1,0:T(8,128)S(1)} %get-tuple-element.23), channel_id=1, replica_groups={{320,336,352,368,384,400,416,432,448,464,480,496,0,16,32,48,64,80,96,11..., dimensions={0} | all-to-all | bytes 524288 | tf_op jit(solution)/shard_map/all_to_all | solution.py:275
  67.0 0.8 suffix.1
  67.7 0.0 copy-done.5
  67.8 8.2 %all-to-all-start.4 = ((f32[32,16,128]{2,1,0:T(8,128)}), f32[32,16,128]{2,1,0:T(8,128)S(1)}, u32[]{:S(2)}, u32[]{:S(2)}) async-start(f32[32,16,128]{2,1,0:T(8,128)} %suffix.1), calls=%async_computation.4 | async-start | bytes 524288 | tf_op jit(solution)/shard_map/all_to_all | solution.py:275
  76.0 0.0 copy-start.6
  76.0 1.0 %copy-done.6 = bf16[512,512]{1,0:T(8,128)(2,1)S(1)} copy-done((bf16[512,512]{1,0:T(8,128)(2,1)S(1)}, bf16[512,512]{1,0:T(8,128)(2,1)}, u32[]{:S(2)}) %copy-start.6) | copy-done | bytes 524312
  77.0 3.4 %local_grads.1 = (bf16[512,512]{1,0:T(8,128)(2,1)}, bf16[512,512]{1,0:T(8,128)(2,1)S(1)}, bf16[512,512]{1,0:T(8,128)(2,1)S(1)}) custom-call(bf16[512,512]{1,0:T(8,128)(2,1)S(1)} %copy-done, bf16[512,512]{1,0:T(8,128)(2,1)S(1)} %copy-done.1, bf16[512,512]{1,0:T(8,128)(2,1)S(1)} %copy-done.2, bf16[512,512]{1,0:T(8,128)(2,1)S(1)} %copy-done.6, ...), custom_call_target="tpu_custom_call" | custom-call | flops 1342177280 | bytes 3948544 | tf_op jit(solution)/shard_map/local_grads/pallas_call | solution.py:249
  80.4 0.0 all-to-all-done.4
  80.4 1.5 %add_carried.1 = (bf16[512,512]{1,0:T(8,128)(2,1)}, bf16[512,512]{1,0:T(8,128)(2,1)}) custom-call(bf16[512,512]{1,0:T(8,128)(2,1)S(1)} %copy-done.1, bf16[512,512]{1,0:T(8,128)(2,1)S(1)} %copy-done.2, f32[8,512]{1,0:T(8,128)S(1)} %get-tuple-element.16.cum_ref, f32[4,128,128]{2,1,0:T(8,128)S(1)} %bitcast.4, ...), custom_call_target="tpu_custom_call" | custom-call | flops 268435456 | bytes 3424256 | tf_op jit(solution)/shard_map/add_carried/pallas_call | solution.py:249
Async XLA Ops:
  0.6 29.3 %copy-start.2 = (bf16[512,512]{1,0:T(8,128)(2,1)S(1)}, bf16[512,512]{1,0:T(8,128)(2,1)}, u32[]{:S(2)}) copy-start(bf16[512,512]{1,0:T(8,128)(2,1)} %values_ref.5) | copy-start | bytes 1572868
  2.8 27.1 %copy-start.1 = (bf16[512,512]{1,0:T(8,128)(2,1)S(1)}, bf16[512,512]{1,0:T(8,128)(2,1)}, u32[]{:S(2)}) copy-start(bf16[512,512]{1,0:T(8,128)(2,1)} %keys_ref.5) | copy-start | bytes 1572868
  20.9 9.0 %copy-start = (bf16[512,512]{1,0:T(8,128)(2,1)S(1)}, bf16[512,512]{1,0:T(8,128)(2,1)}, u32[]{:S(2)}) copy-start(bf16[512,512]{1,0:T(8,128)(2,1)} %queries_ref.7) | copy-start | bytes 1572868
  21.8 12.3 %all-to-all-start.1 = ((f32[32,16,128]{2,1,0:T(8,128)}), f32[32,16,128]{2,1,0:T(8,128)S(1)}, u32[]{:S(2)}, u32[]{:S(2)}) async-start(f32[32,16,128]{2,1,0:T(8,128)} %get-tuple-element.18), calls=%async_computation.1 | async-start | bytes 524288 | tf_op jit(solution)/shard_map/all_to_all | solution.py:275
  30.0 4.1 %copy-start.3 = (bf16[512,512]{1,0:T(8,128)(2,1)S(1)}, bf16[512,512]{1,0:T(8,128)(2,1)}, u32[]{:S(2)}) copy-start(bf16[512,512]{1,0:T(8,128)(2,1)} %upstream_ref.3) | copy-start | bytes 1572868
  31.6 2.4 %copy-start.4 = (f32[512]{0:T(512)S(1)}, f32[512]{0:T(512)}, u32[]{:S(2)}) copy-start(f32[512]{0:T(512)} %param.10) | copy-start | bytes 6148
  53.8 14.0 %copy-start.5 = (bf16[512,512]{1,0:T(8,128)(2,1)}, bf16[512,512]{1,0:T(8,128)(2,1)S(1)}, u32[]{:S(2)}) copy-start(bf16[512,512]{1,0:T(8,128)(2,1)S(1)} %get-tuple-element.21.grad_ref) | copy-start | bytes 1572868
  67.8 12.6 %all-to-all-start.4 = ((f32[32,16,128]{2,1,0:T(8,128)}), f32[32,16,128]{2,1,0:T(8,128)S(1)}, u32[]{:S(2)}, u32[]{:S(2)}) async-start(f32[32,16,128]{2,1,0:T(8,128)} %suffix.1), calls=%async_computation.4 | async-start | bytes 524288 | tf_op jit(solution)/shard_map/all_to_all | solution.py:275
  76.0 1.0 %copy-start.6 = (bf16[512,512]{1,0:T(8,128)(2,1)S(1)}, bf16[512,512]{1,0:T(8,128)(2,1)}, u32[]{:S(2)}) copy-start(bf16[512,512]{1,0:T(8,128)(2,1)} %copy-done.5) | copy-start | bytes 1572868

commit v5 on v4

--- a/solution.py
+++ b/solution.py
@@ -61,7 +61,8 @@
 
 
 def local_states(
-    log_decay_hbm, keys_hbm, values_hbm, out_ref, cum_ref, log_decay_ref, keys_ref, values_ref, sems
+    log_decay_hbm, keys_hbm, values_hbm, out_ref, cum_ref,
+    log_decay_ref, keys_ref, values_ref, weighted_ref, sems,
 ):
     loads = []
     for i, (source, target) in enumerate(
@@ -86,14 +87,14 @@
         total = parts[-1][:, TILE - 1:TILE]
     cumulative = jnp.concatenate(parts, axis=1)
     ending = jnp.exp(total - cumulative)
-    both = jnp.concatenate([cumulative, ending], axis=0)
-    cum_ref[...] = both
-    columns = both.T
+    cum_ref[...] = jnp.concatenate([cumulative, ending], axis=0)
     loads[1].wait()
+    for h in range(heads):
+        weighted = keys_ref[:, head_cols(h)].T.astype(F32) * ending[h:h + 1]
+        weighted_ref[h] = weighted.astype(BF16)
     loads[2].wait()
     for h in range(heads):
-        weighted = keys_ref[:, head_cols(h)].astype(F32) * columns[:, heads + h:heads + h + 1]
-        state = dot(weighted.astype(BF16), values_ref[:, head_cols(h)], (0, 0))
+        state = dot(weighted_ref[h], values_ref[:, head_cols(h)], (1, 0))
         pieces = slice(h * per_head, (h + 1) * per_head)
         out_ref[pieces, :rows, 0, :] = state.reshape(per_head, rows, HEAD_DIM)
         out_ref[pieces, rows, 0, :] = jnp.broadcast_to(total[h:h + 1], (per_head, HEAD_DIM))
@@ -126,12 +127,18 @@
             running = decays_ref[i:i + 1] * running + members_ref[i]
 
 
-def local_attention(queries_ref, keys_ref, values_ref, cum_ref, local_ref):
+def local_attention(
+    queries_ref, keys_ref, values_ref, cum_ref, gain_ref, local_ref, weighted_ref, gain_out_ref
+):
+    gain_out_ref[...] = gain_ref[...]
     heads = local_ref.shape[1] // HEAD_DIM
     cumulative = cum_ref[...]
     columns = cumulative.T
-    for h in range(heads):
-        cols = head_cols(h)
+    growth = jnp.exp(cumulative)
+    for h in range(heads):
+        cols = head_cols(h)
+        weighted = queries_ref[:, cols].T.astype(F32) * growth[h:h + 1]
+        weighted_ref[h] = weighted.astype(BF16)
         for start in range(0, BLK, HALF):
             width = start + HALF
             scores = dot(queries_ref[start:width, cols], keys_ref[:width, cols], (1, 1))
@@ -164,9 +171,7 @@
         sums_ref[d] = sums
 
 
-def grad_states(
-    width, sums_ref, att_ref, upstream_ref, gain_ref, queries_ref, cum_ref, grad_ref, out_ref
-):
+def grad_states(width, sums_ref, att_ref, upstream_ref, gain_ref, weighted_ref, grad_ref, out_ref):
     devices = out_ref.shape[0]
     rows = piece_rows(devices)
     per_head = HEAD_DIM // rows
@@ -176,16 +181,16 @@
     inverse = lax.rsqrt(sums[:tiles] / width + EPSILON)
     pull = inverse * inverse * inverse * sums[tiles:] / width
     scales = jnp.concatenate([inverse, pull], axis=0).T
-    columns = jnp.exp(cum_ref[...]).T
-    for h in range(heads):
-        cols = head_cols(h)
+    for h in range(heads):
+        cols = head_cols(h)
+        grads = []
         for j in range(tiles):
             part = slice(j * TILE, (j + 1) * TILE)
             scaled = gain_ref[:, cols] * upstream_ref[part, cols].astype(F32)
             grad = scales[:, j:j + 1] * scaled - att_ref[part, cols] * scales[:, tiles + j:tiles + j + 1]
-            grad_ref[part, cols] = grad.astype(BF16)
-        weighted = queries_ref[:, cols].astype(F32) * columns[:, h:h + 1]
-        state = dot(weighted.astype(BF16), grad_ref[:, cols], (0, 0))
+            grads.append(grad.astype(BF16))
+            grad_ref[part, cols] = grads[-1]
+        state = dot(weighted_ref[h], jnp.concatenate(grads, axis=0), (1, 0))
         out_ref[h * per_head:(h + 1) * per_head] = state.reshape(per_head, rows, HEAD_DIM)
 
 
@@ -285,13 +290,15 @@
             pltpu.VMEM((heads, tokens), F32),
             pltpu.VMEM(wide, BF16),
             pltpu.VMEM(wide, BF16),
+            pltpu.VMEM((heads, HEAD_DIM, tokens), BF16),
             pltpu.SemaphoreType.DMA((3,)),
         ],
     )
     members = exchange(pieces, "ctx")
-    local = call(
-        local_attention, "local_attention", f32(wide),
-        queries, keys, values, cumulative, flops=2 * square,
+    local, weighted, gain = call(
+        local_attention, "local_attention",
+        (f32(wide), pltpu.HBM((heads, HEAD_DIM, tokens), BF16), f32((1, columns))),
+        queries, keys, values, cumulative, gain, flops=2 * square,
     )
     starts, decays = call(
         prefix, "prefix", (f32((slabs, rows, HEAD_DIM)), f32((slabs, HEAD_DIM))), members
@@ -305,7 +312,7 @@
     grad_out, grad_pieces = call(
         functools.partial(grad_states, full_width), "grad_states",
         (bf16(wide), f32((slabs, rows, HEAD_DIM))),
-        sums, attended, upstream, gain, queries, cumulative, flops=square // 4,
+        sums, attended, upstream, gain, weighted, flops=square // 4,
     )
     grad_members = exchange(grad_pieces, "ctx")
     grad_queries, local_keys, local_values = call(

time: 82.3 us -> 81.6 us (level)
  waiting for transfers between devices: 2.43 us -> 1.03 us
    all_to_all x2, waiting for transfers between devices: 2.43 us -> 1.03 us  [exchange(): return lax.all_to_all(x, axis, 0, 0, tiled=True, axis_index_groups=[order])]
    unnamed x14 -> x16, local copies, waits for them, and re-layouts: 1.07 us -> 1.71 us
  transfers between devices with their start and end apart: 2 -> 2, of which waited for: 1 -> 1; matrix products, arithmetic and copies ran while one was open for 0% -> 0% of each run, Pallas kernels for 6% -> 7%
where the time goes in v5:
time: 81.6 us; the launch traced here: 81.1 us
  blocking collectives  49.2 us (60%)
  starting transfers between devices  16.3 us (20%)
  Pallas kernels  12.1 us (15%)
  local copies, waits for them, and re-layouts  1.71 us (2%)
  waiting for transfers between devices  1.03 us (1%)
    all_to_all x3, blocking collectives, exchange(): return lax.all_to_all(x, axis, 0, 0, tiled=True, axis_index_groups=[order])  49.2 us
    all_to_all x2, starting transfers between devices, exchange(): return lax.all_to_all(x, axis, 0, 0, tiled=True, axis_index_groups=[order])  16.3 us
    pallas_call x8, Pallas kernels, call(): pl.pallas_call(kernel, out_shape=out_shape, name=name, compiler_params=pl...  12.1 us
    unnamed x16, local copies, waits for them, and re-layouts  1.71 us
  transfers between devices with their start and end apart: 2, of which 1 were waited for; matrix products, arithmetic and copies ran while one was open for 0% of the time, Pallas kernels for 7%

profile of v5, /device:TPU:1, one launch (start us, length us, event | category | flops | bytes accessed | tf_op | source)
XLA Modules:
  0.0 81.1 jit_solution(12601641292346852715)
XLA Ops:
  0.6 0.0 copy-start.4
  0.6 1.8 %local_states.1 = (f32[32,17,1,128]{3,2,1,0:T(1,128)S(1)}, f32[8,512]{1,0:T(8,128)S(1)}) custom-call(f32[4,512]{1,0:T(4,128)} %bitcast.8, bf16[512,512]{1,0:T(8,128)(2,1)} %keys_ref.5, bf16[512,512]{1,0:T(8,128)(2,1)} %values_ref.5), custom_call_target="tpu_custom_call" | custom-call | flops 67108864 | bytes 1351680 | tf_op jit(solution)/shard_map/local_states/pallas_call | solution.py:254
  2.4 0.0 copy-start.2
  2.5 18.1 %all_to_all.25.members_ref = f32[32,17,1,128]{3,2,1,0:T(1,128)S(1)} all-to-all(f32[32,17,1,128]{3,2,1,0:T(1,128)S(1)} %get-tuple-element.22), channel_id=1, replica_groups={{320,336,352,368,384,400,416,432,448,464,480,496,0,16,32,48,64,80,96,11..., dimensions={0} | all-to-all | bytes 557056 | tf_op jit(solution)/shard_map/all_to_all | solution.py:280
  20.6 0.0 copy-start.1
  20.6 0.9 %prefix.1 = (f32[32,16,128]{2,1,0:T(8,128)}, f32[32,128]{1,0:T(8,128)S(1)}) custom-call(f32[32,17,1,128]{3,2,1,0:T(1,128)S(1)} %all_to_all.25.members_ref), custom_call_target="tpu_custom_call" | custom-call | bytes 557056 | tf_op jit(solution)/shard_map/prefix/pallas_call | solution.py:254
  21.4 8.1 %all-to-all-start.1 = ((f32[32,16,128]{2,1,0:T(8,128)}), f32[32,16,128]{2,1,0:T(8,128)S(1)}, u32[]{:S(2)}, u32[]{:S(2)}) async-start(f32[32,16,128]{2,1,0:T(8,128)} %get-tuple-element.23), calls=%async_computation.1 | async-start | bytes 524288 | tf_op jit(solution)/shard_map/all_to_all | solution.py:280
  29.6 0.0 copy-start.7
  29.6 0.0 copy-done.4
  29.6 0.0 copy-done.2
  29.6 0.0 copy-done.1
  29.6 0.6 copy-done.7
  30.2 0.0 copy-start
  30.2 2.4 %local_attention.1 = (f32[512,512]{1,0:T(8,128)S(1)}, bf16[4,128,512]{2,1,0:T(8,128)(2,1)}, f32[1,512]{1,0:T(1,128)S(1)}) custom-call(bf16[512,512]{1,0:T(8,128)(2,1)S(1)} %copy-done.4, bf16[512,512]{1,0:T(8,128)(2,1)S(1)} %copy-done.1, bf16[512,512]{1,0:T(8,128)(2,1)S(1)} %copy-done.2, f32[8,512]{1,0:T(8,128)S(1)} %get-tuple-element.19.cum_ref, ...), custom_call_target="tpu_custom_call" | custom-call | flops 536870912 | bytes 3166208 | tf_op jit(solution)/shard_map/local_attention/pallas_call | solution.py:254
  32.7 1.0 %all-to-all-done.1 = f32[32,16,128]{2,1,0:T(8,128)S(1)} async-done(((f32[32,16,128]{2,1,0:T(8,128)}), f32[32,16,128]{2,1,0:T(8,128)S(1)}, u32[]{:S(2)}, u32[]{:S(2)}) %all-to-all-start.1) | async-done | bytes 262176 | tf_op jit(solution)/shard_map/all_to_all | solution.py:280
  33.7 0.0 copy-done
  33.7 0.0 copy-start.3
  33.7 0.7 attend.1
  34.4 17.8 %all_to_all.26.sums_ref = f32[16,8,128]{2,1,0:T(8,128)S(1)} all-to-all(f32[16,8,128]{2,1,0:T(8,128)S(1)} %get-tuple-element.24), channel_id=1, replica_groups={{10,11,12,13,14,15,0,1,2,3,4,5,6,7,8,9},{26,27,28,29,30,31,16,17,18,19,..., dimensions={0} | all-to-all | bytes 131072 | tf_op jit(solution)/shard_map/all_to_all | solution.py:280
  52.2 0.0 copy-done.3
  52.2 0.7 grad_states.1
  52.9 0.0 copy-start.5
  52.9 13.3 %all_to_all.27.members_ref = f32[32,16,128]{2,1,0:T(8,128)S(1)} all-to-all(f32[32,16,128]{2,1,0:T(8,128)S(1)} %get-tuple-element.29), channel_id=1, replica_groups={{320,336,352,368,384,400,416,432,448,464,480,496,0,16,32,48,64,80,96,11..., dimensions={0} | all-to-all | bytes 524288 | tf_op jit(solution)/shard_map/all_to_all | solution.py:280
  66.2 0.0 copy-done.5
  66.2 0.8 suffix.1
  67.0 8.2 %all-to-all-start.4 = ((f32[32,16,128]{2,1,0:T(8,128)}), f32[32,16,128]{2,1,0:T(8,128)S(1)}, u32[]{:S(2)}, u32[]{:S(2)}) async-start(f32[32,16,128]{2,1,0:T(8,128)} %suffix.1), calls=%async_computation.4 | async-start | bytes 524288 | tf_op jit(solution)/shard_map/all_to_all | solution.py:280
  75.2 0.0 copy-start.6
  75.2 1.0 %copy-done.6 = bf16[512,512]{1,0:T(8,128)(2,1)S(1)} copy-done((bf16[512,512]{1,0:T(8,128)(2,1)S(1)}, bf16[512,512]{1,0:T(8,128)(2,1)}, u32[]{:S(2)}) %copy-start.6) | copy-done | bytes 524312
  76.2 3.4 %local_grads.1 = (bf16[512,512]{1,0:T(8,128)(2,1)}, bf16[512,512]{1,0:T(8,128)(2,1)S(1)}, bf16[512,512]{1,0:T(8,128)(2,1)S(1)}) custom-call(bf16[512,512]{1,0:T(8,128)(2,1)S(1)} %copy-done.4, bf16[512,512]{1,0:T(8,128)(2,1)S(1)} %copy-done.1, bf16[512,512]{1,0:T(8,128)(2,1)S(1)} %copy-done.2, bf16[512,512]{1,0:T(8,128)(2,1)S(1)} %copy-done.6, ...), custom_call_target="tpu_custom_call" | custom-call | flops 1342177280 | bytes 3948544 | tf_op jit(solution)/shard_map/local_grads/pallas_call | solution.py:254
  79.6 0.0 all-to-all-done.4
  79.6 1.5 %add_carried.1 = (bf16[512,512]{1,0:T(8,128)(2,1)}, bf16[512,512]{1,0:T(8,128)(2,1)}) custom-call(bf16[512,512]{1,0:T(8,128)(2,1)S(1)} %copy-done.1, bf16[512,512]{1,0:T(8,128)(2,1)S(1)} %copy-done.2, f32[8,512]{1,0:T(8,128)S(1)} %get-tuple-element.19.cum_ref, f32[4,128,128]{2,1,0:T(8,128)S(1)} %bitcast.4, ...), custom_call_target="tpu_custom_call" | custom-call | flops 268435456 | bytes 3424256 | tf_op jit(solution)/shard_map/add_carried/pallas_call | solution.py:254
Async XLA Ops:
  0.6 28.9 %copy-start.4 = (bf16[512,512]{1,0:T(8,128)(2,1)S(1)}, bf16[512,512]{1,0:T(8,128)(2,1)}, u32[]{:S(2)}) copy-start(bf16[512,512]{1,0:T(8,128)(2,1)} %queries_ref.5) | copy-start | bytes 1572868
  2.4 27.1 %copy-start.2 = (bf16[512,512]{1,0:T(8,128)(2,1)S(1)}, bf16[512,512]{1,0:T(8,128)(2,1)}, u32[]{:S(2)}) copy-start(bf16[512,512]{1,0:T(8,128)(2,1)} %values_ref.5) | copy-start | bytes 1572868
  20.6 9.0 %copy-start.1 = (bf16[512,512]{1,0:T(8,128)(2,1)S(1)}, bf16[512,512]{1,0:T(8,128)(2,1)}, u32[]{:S(2)}) copy-start(bf16[512,512]{1,0:T(8,128)(2,1)} %keys_ref.5) | copy-start | bytes 1572868
  21.4 12.3 %all-to-all-start.1 = ((f32[32,16,128]{2,1,0:T(8,128)}), f32[32,16,128]{2,1,0:T(8,128)S(1)}, u32[]{:S(2)}, u32[]{:S(2)}) async-start(f32[32,16,128]{2,1,0:T(8,128)} %get-tuple-element.23), calls=%async_computation.1 | async-start | bytes 524288 | tf_op jit(solution)/shard_map/all_to_all | solution.py:280
  29.6 0.7 copy-start.7
  30.2 3.5 %copy-start = (bf16[512,512]{1,0:T(8,128)(2,1)S(1)}, bf16[512,512]{1,0:T(8,128)(2,1)}, u32[]{:S(2)}) copy-start(bf16[512,512]{1,0:T(8,128)(2,1)} %upstream_ref.3) | copy-start | bytes 1572868
  33.7 18.5 %copy-start.3 = (bf16[4,128,512]{2,1,0:T(8,128)(2,1)S(1)}, bf16[4,128,512]{2,1,0:T(8,128)(2,1)}, u32[]{:S(2)}) copy-start(bf16[4,128,512]{2,1,0:T(8,128)(2,1)} %get-tuple-element.26.weighted_ref) | copy-start | bytes 1572868
  52.9 13.3 %copy-start.5 = (bf16[512,512]{1,0:T(8,128)(2,1)}, bf16[512,512]{1,0:T(8,128)(2,1)S(1)}, u32[]{:S(2)}) copy-start(bf16[512,512]{1,0:T(8,128)(2,1)S(1)} %get-tuple-element.27.grad_ref) | copy-start | bytes 1572868
  67.0 12.6 %all-to-all-start.4 = ((f32[32,16,128]{2,1,0:T(8,128)}), f32[32,16,128]{2,1,0:T(8,128)S(1)}, u32[]{:S(2)}, u32[]{:S(2)}) async-start(f32[32,16,128]{2,1,0:T(8,128)} %suffix.1), calls=%async_computation.4 | async-start | bytes 524288 | tf_op jit(solution)/shard_map/all_to_all | solution.py:280
  75.2 1.0 %copy-start.6 = (bf16[512,512]{1,0:T(8,128)(2,1)S(1)}, bf16[512,512]{1,0:T(8,128)(2,1)}, u32[]{:S(2)}) copy-start(bf16[512,512]{1,0:T(8,128)(2,1)} %copy-done.5) | copy-start | bytes 1572868

commit v6 on v5

--- a/solution.py
+++ b/solution.py
@@ -116,7 +116,8 @@
             running = decays_ref[i:i + 1] * running + members_ref[i, :rows, 0, :]
 
 
-def suffix(members_ref, decays_ref, out_ref):
+def suffix(members_ref, decays_ref, out_ref, after_ref):
+    after_ref[...] = decays_ref[:1]
     devices, rows = out_ref.shape[:2]
     order = rotated(devices)
     running = jnp.zeros((rows, HEAD_DIM), F32)
@@ -194,30 +195,45 @@
         out_ref[h * per_head:(h + 1) * per_head] = state.reshape(per_head, rows, HEAD_DIM)
 
 
-def local_grads(
-    queries_ref, keys_ref, values_ref, grad_ref, cum_ref, state_ref,
-    grad_queries_ref, grad_keys_ref, grad_values_ref,
-):
-    heads = state_ref.shape[0]
+def mix(
+    queries_ref, keys_ref, grad_ref, cum_ref, state_ref, after_ref,
+    mixing_ref, carried_ref, copy_ref,
+):
+    del after_ref
+    copy_ref[...] = grad_ref[...]
     cumulative = cum_ref[...]
     columns = cumulative.T
-    for h in range(heads):
-        cols = head_cols(h)
+    for h in range(mixing_ref.shape[0]):
+        cols = head_cols(h)
+        for start in range(0, BLK, HALF):
+            stop = start + HALF
+            scores = dot(queries_ref[start:stop, cols], keys_ref[:stop, cols], (1, 1))
+            decays = decay_tile(cumulative, columns, h, start)
+            mixing_ref[h, start:stop, :stop] = (scores * decays).astype(BF16)
         high, low = split(state_ref[h])
-        both = jnp.concatenate([high, low], axis=1)
+        carried = dot(twice(grad_ref[:, cols]), jnp.concatenate([high, low], axis=1), (1, 1))
+        carried_ref[:, cols] = jnp.exp(columns[:, h:h + 1]) * carried
+
+
+def local_grads(
+    queries_ref, keys_ref, values_ref, grad_ref, cum_ref, mixing_ref, carried_ref,
+    grad_queries_ref, grad_keys_ref, grad_values_ref,
+):
+    heads = mixing_ref.shape[0]
+    cumulative = cum_ref[...]
+    columns = cumulative.T
+    for h in range(heads):
+        cols = head_cols(h)
         key_sums, value_sums = [], []
         for start in range(0, BLK, HALF):
             stop = start + HALF
             grad = grad_ref[start:stop, cols]
-            query = queries_ref[start:stop, cols]
             decays = decay_tile(cumulative, columns, h, start)
-            mixing = (dot(query, keys_ref[:stop, cols], (1, 1)) * decays).astype(BF16)
             grad_mixing = (dot(grad, values_ref[:stop, cols], (1, 1)) * decays).astype(BF16)
-            carried = jnp.exp(columns[start:stop, h:h + 1]) * dot(twice(grad), both, (1, 1))
-            grad_query = carried + dot(grad_mixing, keys_ref[:stop, cols], (1, 0))
+            grad_query = carried_ref[start:stop, cols] + dot(grad_mixing, keys_ref[:stop, cols], (1, 0))
             grad_queries_ref[start:stop, cols] = grad_query.astype(BF16)
-            key_sums.append(dot(query, grad_mixing, (0, 0)))
-            value_sums.append(dot(grad, mixing, (0, 0)))
+            key_sums.append(dot(queries_ref[start:stop, cols], grad_mixing, (0, 0)))
+            value_sums.append(dot(grad, mixing_ref[h, start:stop, :stop], (0, 0)))
         grad_keys_ref[:, cols] = add_halves(*key_sums).T.astype(BF16)
         grad_values_ref[:, cols] = add_halves(*value_sums).T.astype(BF16)
 
@@ -315,11 +331,17 @@
         sums, attended, upstream, gain, weighted, flops=square // 4,
     )
     grad_members = exchange(grad_pieces, "ctx")
+    ends, after = call(
+        suffix, "suffix", (f32((slabs, rows, HEAD_DIM)), f32((1, HEAD_DIM))), grad_members, decays
+    )
+    mixing, carried, grad_out = call(
+        mix, "mix", (bf16((heads, tokens, tokens)), f32(wide), bf16(wide)),
+        queries, keys, grad_out, cumulative, start_state, after, flops=2 * square,
+    )
     grad_queries, local_keys, local_values = call(
         local_grads, "local_grads", (bf16(wide), bf16(wide), bf16(wide)),
-        queries, keys, values, grad_out, cumulative, start_state, flops=5 * square,
-    )
-    ends = call(suffix, "suffix", f32((slabs, rows, HEAD_DIM)), grad_members, decays)
+        queries, keys, values, grad_out, cumulative, mixing, carried, flops=4 * square,
+    )
     end_state = exchange(ends, "ctx").reshape(heads, HEAD_DIM, HEAD_DIM)
     grad_keys, grad_values = call(
         add_carried, "add_carried", (bf16(wide), bf16(wide)),

time: 81.6 us -> 81.2 us (level)
  local copies, waits for them, and re-layouts: 1.71 us -> 0.02 us
    unnamed x16 -> x12, local copies, waits for them, and re-layouts: 1.71 us -> 0.02 us
    pallas_call x8 -> x9, Pallas kernels: 12.1 us -> 12.9 us  [call(): pl.pallas_call(kernel, out_shape=out_shape, name=name, compiler_params=pl...]
  transfers between devices with their start and end apart: 2 -> 2, of which waited for: 1 -> 2; matrix products, arithmetic and copies ran while one was open for 0% -> 0% of each run, Pallas kernels for 7% -> 8%
where the time goes in v6:
time: 81.2 us; the launch traced here: 80.8 us
  blocking collectives  49.1 us (60%)
  starting transfers between devices  16.3 us (20%)
  Pallas kernels  12.9 us (16%)
  waiting for transfers between devices  1.73 us (2%)
    all_to_all x3, blocking collectives, exchange(): return lax.all_to_all(x, axis, 0, 0, tiled=True, axis_index_groups=[order])  49.1 us
    all_to_all x2, starting transfers between devices, exchange(): return lax.all_to_all(x, axis, 0, 0, tiled=True, axis_index_groups=[order])  16.3 us
    pallas_call x9, Pallas kernels, call(): pl.pallas_call(kernel, out_shape=out_shape, name=name, compiler_params=pl...  12.9 us
    all_to_all x2, waiting for transfers between devices, exchange(): return lax.all_to_all(x, axis, 0, 0, tiled=True, axis_index_groups=[order])  1.73 us
  transfers between devices with their start and end apart: 2, of which 2 were waited for; matrix products, arithmetic and copies ran while one was open for 0% of the time, Pallas kernels for 8%

profile of v6, /device:TPU:1, one launch (start us, length us, event | category | flops | bytes accessed | tf_op | source)
XLA Modules:
  0.0 80.8 jit_solution(1803629132708586250)
XLA Ops:
  0.6 0.0 copy-start
  0.6 0.0 copy-start.1
  0.7 0.0 copy-start.3
  0.7 0.0 copy-start.5
  0.7 0.0 copy-start.2
  0.7 1.9 %local_states.1 = (f32[32,17,1,128]{3,2,1,0:T(1,128)S(1)}, f32[8,512]{1,0:T(8,128)S(1)}) custom-call(f32[4,512]{1,0:T(4,128)} %bitcast.8, bf16[512,512]{1,0:T(8,128)(2,1)} %keys_ref.7, bf16[512,512]{1,0:T(8,128)(2,1)} %values_ref.5), custom_call_target="tpu_custom_call" | custom-call | flops 67108864 | bytes 1351680 | tf_op jit(solution)/shard_map/local_states/pallas_call | solution.py:270
  2.6 18.0 %all_to_all.25.members_ref = f32[32,17,1,128]{3,2,1,0:T(1,128)S(1)} all-to-all(f32[32,17,1,128]{3,2,1,0:T(1,128)S(1)} %get-tuple-element.27), channel_id=1, replica_groups={{320,336,352,368,384,400,416,432,448,464,480,496,0,16,32,48,64,80,96,11..., dimensions={0} | all-to-all | bytes 557056 | tf_op jit(solution)/shard_map/all_to_all | solution.py:296
  20.6 0.9 %prefix.1 = (f32[32,16,128]{2,1,0:T(8,128)}, f32[32,128]{1,0:T(8,128)S(1)}) custom-call(f32[32,17,1,128]{3,2,1,0:T(1,128)S(1)} %all_to_all.25.members_ref), custom_call_target="tpu_custom_call" | custom-call | bytes 557056 | tf_op jit(solution)/shard_map/prefix/pallas_call | solution.py:270
  21.4 8.1 %all-to-all-start.1 = ((f32[32,16,128]{2,1,0:T(8,128)}), f32[32,16,128]{2,1,0:T(8,128)S(1)}, u32[]{:S(2)}, u32[]{:S(2)}) async-start(f32[32,16,128]{2,1,0:T(8,128)} %get-tuple-element.28), calls=%async_computation.1 | async-start | bytes 524288 | tf_op jit(solution)/shard_map/all_to_all | solution.py:296
  29.5 0.0 copy-done
  29.6 0.0 copy-done.1
  29.6 0.0 copy-done.3
  29.6 0.0 copy-done.5
  29.6 2.4 %local_attention.1 = (f32[512,512]{1,0:T(8,128)S(1)}, bf16[4,128,512]{2,1,0:T(8,128)(2,1)}, f32[1,512]{1,0:T(1,128)S(1)}) custom-call(bf16[512,512]{1,0:T(8,128)(2,1)S(1)} %copy-done.3, bf16[512,512]{1,0:T(8,128)(2,1)S(1)} %copy-done, bf16[512,512]{1,0:T(8,128)(2,1)S(1)} %copy-done.1, f32[8,512]{1,0:T(8,128)S(1)} %get-tuple-element.24.cum_ref, ...), custom_call_target="tpu_custom_call" | custom-call | flops 536870912 | bytes 3166208 | tf_op jit(solution)/shard_map/local_attention/pallas_call | solution.py:270
  32.0 1.7 %all-to-all-done.1 = f32[32,16,128]{2,1,0:T(8,128)S(1)} async-done(((f32[32,16,128]{2,1,0:T(8,128)}), f32[32,16,128]{2,1,0:T(8,128)S(1)}, u32[]{:S(2)}, u32[]{:S(2)}) %all-to-all-start.1) | async-done | bytes 262176 | tf_op jit(solution)/shard_map/all_to_all | solution.py:296
  33.7 0.0 copy-start.4
  33.7 0.0 copy-done.2
  33.7 0.7 attend.1
  34.4 17.9 %all_to_all.26.sums_ref = f32[16,8,128]{2,1,0:T(8,128)S(1)} all-to-all(f32[16,8,128]{2,1,0:T(8,128)S(1)} %get-tuple-element.29), channel_id=1, replica_groups={{10,11,12,13,14,15,0,1,2,3,4,5,6,7,8,9},{26,27,28,29,30,31,16,17,18,19,..., dimensions={0} | all-to-all | bytes 131072 | tf_op jit(solution)/shard_map/all_to_all | solution.py:296
  52.3 0.0 copy-done.4
  52.3 0.7 grad_states.1
  53.0 13.2 %all_to_all.27.members_ref = f32[32,16,128]{2,1,0:T(8,128)S(1)} all-to-all(f32[32,16,128]{2,1,0:T(8,128)S(1)} %get-tuple-element.33), channel_id=1, replica_groups={{320,336,352,368,384,400,416,432,448,464,480,496,0,16,32,48,64,80,96,11..., dimensions={0} | all-to-all | bytes 524288 | tf_op jit(solution)/shard_map/all_to_all | solution.py:296
  66.2 0.8 suffix.1
  67.0 8.2 %all-to-all-start.4 = ((f32[32,16,128]{2,1,0:T(8,128)}), f32[32,16,128]{2,1,0:T(8,128)S(1)}, u32[]{:S(2)}, u32[]{:S(2)}) async-start(f32[32,16,128]{2,1,0:T(8,128)} %get-tuple-element.40), calls=%async_computation.4 | async-start | bytes 524288 | tf_op jit(solution)/shard_map/all_to_all | solution.py:296
  75.1 1.0 %mix.1 = (bf16[4,512,512]{2,1,0:T(8,128)(2,1)S(1)}, f32[512,512]{1,0:T(8,128)S(1)}, bf16[512,512]{1,0:T(8,128)(2,1)S(1)}) custom-call(bf16[512,512]{1,0:T(8,128)(2,1)S(1)} %copy-done.3, bf16[512,512]{1,0:T(8,128)(2,1)S(1)} %copy-done, bf16[512,512]{1,0:T(8,128)(2,1)S(1)} %get-tuple-element.32.grad_ref, f32[8,512]{1,0:T(8,128)S(1)} %get-tuple-element.24.cum_ref, ...), custom_call_target="tpu_custom_call" | custom-call | flops 536870912 | bytes 5521920 | tf_op jit(solution)/shard_map/mix/pallas_call | solution.py:270
  76.2 3.0 %local_grads.1 = (bf16[512,512]{1,0:T(8,128)(2,1)}, bf16[512,512]{1,0:T(8,128)(2,1)S(1)}, bf16[512,512]{1,0:T(8,128)(2,1)S(1)}) custom-call(bf16[512,512]{1,0:T(8,128)(2,1)S(1)} %copy-done.3, bf16[512,512]{1,0:T(8,128)(2,1)S(1)} %copy-done, bf16[512,512]{1,0:T(8,128)(2,1)S(1)} %copy-done.1, bf16[512,512]{1,0:T(8,128)(2,1)S(1)} %get-tuple-element.36.grad_ref, ...), custom_call_target="tpu_custom_call" | custom-call | flops 1073741824 | bytes 6832128 | tf_op jit(solution)/shard_map/local_grads/pallas_call | solution.py:270
  79.2 0.1 all-to-all-done.4
  79.3 1.5 %add_carried.1 = (bf16[512,512]{1,0:T(8,128)(2,1)}, bf16[512,512]{1,0:T(8,128)(2,1)}) custom-call(bf16[512,512]{1,0:T(8,128)(2,1)S(1)} %copy-done, bf16[512,512]{1,0:T(8,128)(2,1)S(1)} %copy-done.1, f32[8,512]{1,0:T(8,128)S(1)} %get-tuple-element.24.cum_ref, f32[4,128,128]{2,1,0:T(8,128)S(1)} %bitcast.4, ...), custom_call_target="tpu_custom_call" | custom-call | flops 268435456 | bytes 3424256 | tf_op jit(solution)/shard_map/add_carried/pallas_call | solution.py:270
Async XLA Ops:
  0.6 28.9 %copy-start = (bf16[512,512]{1,0:T(8,128)(2,1)S(1)}, bf16[512,512]{1,0:T(8,128)(2,1)}, u32[]{:S(2)}) copy-start(bf16[512,512]{1,0:T(8,128)(2,1)} %keys_ref.7) | copy-start | bytes 1572868
  0.6 28.9 %copy-start.1 = (bf16[512,512]{1,0:T(8,128)(2,1)S(1)}, bf16[512,512]{1,0:T(8,128)(2,1)}, u32[]{:S(2)}) copy-start(bf16[512,512]{1,0:T(8,128)(2,1)} %values_ref.5) | copy-start | bytes 1572868
  0.7 28.9 %copy-start.3 = (bf16[512,512]{1,0:T(8,128)(2,1)S(1)}, bf16[512,512]{1,0:T(8,128)(2,1)}, u32[]{:S(2)}) copy-start(bf16[512,512]{1,0:T(8,128)(2,1)} %queries_ref.7) | copy-start | bytes 1572868
  0.7 28.9 %copy-start.5 = (f32[512]{0:T(512)S(1)}, f32[512]{0:T(512)}, u32[]{:S(2)}) copy-start(f32[512]{0:T(512)} %param.10) | copy-start | bytes 6148
  0.7 33.0 %copy-start.2 = (bf16[512,512]{1,0:T(8,128)(2,1)S(1)}, bf16[512,512]{1,0:T(8,128)(2,1)}, u32[]{:S(2)}) copy-start(bf16[512,512]{1,0:T(8,128)(2,1)} %upstream_ref.3) | copy-start | bytes 1572868
  21.4 12.3 %all-to-all-start.1 = ((f32[32,16,128]{2,1,0:T(8,128)}), f32[32,16,128]{2,1,0:T(8,128)S(1)}, u32[]{:S(2)}, u32[]{:S(2)}) async-start(f32[32,16,128]{2,1,0:T(8,128)} %get-tuple-element.28), calls=%async_computation.1 | async-start | bytes 524288 | tf_op jit(solution)/shard_map/all_to_all | solution.py:296
  33.7 18.6 %copy-start.4 = (bf16[4,128,512]{2,1,0:T(8,128)(2,1)S(1)}, bf16[4,128,512]{2,1,0:T(8,128)(2,1)}, u32[]{:S(2)}) copy-start(bf16[4,128,512]{2,1,0:T(8,128)(2,1)} %get-tuple-element.31.weighted_ref) | copy-start | bytes 1572868
  67.0 12.3 %all-to-all-start.4 = ((f32[32,16,128]{2,1,0:T(8,128)}), f32[32,16,128]{2,1,0:T(8,128)S(1)}, u32[]{:S(2)}, u32[]{:S(2)}) async-start(f32[32,16,128]{2,1,0:T(8,128)} %get-tuple-element.40), calls=%async_computation.4 | async-start | bytes 524288 | tf_op jit(solution)/shard_map/all_to_all | solution.py:296

commit v7 on v6

--- a/solution.py
+++ b/solution.py
@@ -104,28 +104,49 @@
     return [(size * 5 // 8 + i) % size for i in range(size)]
 
 
-def prefix(members_ref, out_ref, decays_ref):
+def send_group(stores, running_ref, out_hbm, sems, first):
+    size = max(1, out_hbm.shape[0] // 8)
+    part = pl.ds(first, size)
+    stores.append(
+        pltpu.make_async_copy(running_ref.at[part], out_hbm.at[part], sems.at[first // size])
+    )
+    stores[-1].start()
+
+
+def prefix(members_ref, out_hbm, decays_ref, out_ref, sems):
     devices, rows = out_ref.shape[:2]
     order = rotated(devices)
+    size = max(1, devices // 8)
+    stores = []
     decays_ref[...] = jnp.exp(members_ref[:, rows, 0, :])
     running = jnp.zeros((rows, HEAD_DIM), F32)
     for b in range(devices):
         i = order.index(b)
         out_ref[i] = running
+        if (b + 1) % size == 0:
+            send_group(stores, out_ref, out_hbm, sems, i // size * size)
         if b < devices - 1:
             running = decays_ref[i:i + 1] * running + members_ref[i, :rows, 0, :]
-
-
-def suffix(members_ref, decays_ref, out_ref, after_ref):
+    for store in stores:
+        store.wait()
+
+
+def suffix(members_ref, decays_ref, out_hbm, after_ref, out_ref, sems):
     after_ref[...] = decays_ref[:1]
     devices, rows = out_ref.shape[:2]
     order = rotated(devices)
+    size = max(1, devices // 8)
+    stores = []
     running = jnp.zeros((rows, HEAD_DIM), F32)
     for b in reversed(range(devices)):
         i = order.index(b)
         out_ref[i] = running
+        if b % size == 0:
+            send_group(stores, out_ref, out_hbm, sems, i // size * size)
         if b > 0:
             running = decays_ref[i:i + 1] * running + members_ref[i]
+    for store in stores:
+        store.wait()
 
 
 def local_attention(
@@ -288,6 +309,7 @@
     f32 = functools.partial(jax.ShapeDtypeStruct, dtype=F32)
     bf16 = functools.partial(jax.ShapeDtypeStruct, dtype=BF16)
     square = tokens * tokens * HEAD_DIM * heads * 2
+    in_vmem = pl.BlockSpec(memory_space=pltpu.VMEM)
     in_hbm = pl.BlockSpec(memory_space=pltpu.HBM)
     wide = (tokens, columns)
 
@@ -317,7 +339,13 @@
         queries, keys, values, cumulative, gain, flops=2 * square,
     )
     starts, decays = call(
-        prefix, "prefix", (f32((slabs, rows, HEAD_DIM)), f32((slabs, HEAD_DIM))), members
+        prefix, "prefix",
+        (pltpu.HBM((slabs, rows, HEAD_DIM), F32), f32((slabs, HEAD_DIM))), members,
+        out_specs=[in_hbm, in_vmem],
+        scratch_shapes=[
+            pltpu.VMEM((slabs, rows, HEAD_DIM), F32),
+            pltpu.SemaphoreType.DMA((8,)),
+        ],
     )
     start_state = exchange(starts, "ctx").reshape(heads, HEAD_DIM, HEAD_DIM)
     attended, sums = call(
@@ -332,7 +360,13 @@
     )
     grad_members = exchange(grad_pieces, "ctx")
     ends, after = call(
-        suffix, "suffix", (f32((slabs, rows, HEAD_DIM)), f32((1, HEAD_DIM))), grad_members, decays
+        suffix, "suffix",
+        (pltpu.HBM((slabs, rows, HEAD_DIM), F32), f32((1, HEAD_DIM))), grad_members, decays,
+        out_specs=[in_hbm, in_vmem],
+        scratch_shapes=[
+            pltpu.VMEM((slabs, rows, HEAD_DIM), F32),
+            pltpu.SemaphoreType.DMA((8,)),
+        ],
     )
     mixing, carried, grad_out = call(
         mix, "mix", (bf16((heads, tokens, tokens)), f32(wide), bf16(wide)),

time: 81.2 us -> 81.2 us (level)
  transfers between devices with their start and end apart: 2 -> 2, of which waited for: 2 -> 1; matrix products, arithmetic and copies ran while one was open for 0% -> 0% of each run, Pallas kernels for 8% -> 8%
where the time goes in v7:
time: 81.2 us; the launch traced here: 80.8 us
  blocking collectives  49.1 us (60%)
  starting transfers between devices  16.3 us (20%)
  Pallas kernels  12.9 us (16%)
  waiting for transfers between devices  1.72 us (2%)
    all_to_all x3, blocking collectives, exchange(): return lax.all_to_all(x, axis, 0, 0, tiled=True, axis_index_groups=[order])  49.1 us
    all_to_all x2, starting transfers between devices, exchange(): return lax.all_to_all(x, axis, 0, 0, tiled=True, axis_index_groups=[order])  16.3 us
    pallas_call x9, Pallas kernels, call(): pl.pallas_call(kernel, out_shape=out_shape, name=name, compiler_params=pl...  12.9 us
    all_to_all x2, waiting for transfers between devices, exchange(): return lax.all_to_all(x, axis, 0, 0, tiled=True, axis_index_groups=[order])  1.72 us
  transfers between devices with their start and end apart: 2, of which 1 were waited for; matrix products, arithmetic and copies ran while one was open for 0% of the time, Pallas kernels for 8%

profile of v7, /device:TPU:1, one launch (start us, length us, event | category | flops | bytes accessed | tf_op | source)
XLA Modules:
  0.0 80.8 jit_solution(11492545767139191072)
XLA Ops:
  0.6 0.0 copy-start
  0.6 0.0 copy-start.1
  0.7 0.0 copy-start.3
  0.7 0.0 copy-start.5
  0.7 0.0 copy-start.2
  0.7 1.9 %local_states.1 = (f32[32,17,1,128]{3,2,1,0:T(1,128)S(1)}, f32[8,512]{1,0:T(8,128)S(1)}) custom-call(f32[4,512]{1,0:T(4,128)} %bitcast.8, bf16[512,512]{1,0:T(8,128)(2,1)} %keys_ref.7, bf16[512,512]{1,0:T(8,128)(2,1)} %values_ref.5), custom_call_target="tpu_custom_call" | custom-call | flops 67108864 | bytes 1351680 | tf_op jit(solution)/shard_map/local_states/pallas_call | solution.py:291
  2.6 18.0 %all_to_all.25.members_ref = f32[32,17,1,128]{3,2,1,0:T(1,128)S(1)} all-to-all(f32[32,17,1,128]{3,2,1,0:T(1,128)S(1)} %get-tuple-element.27), channel_id=1, replica_groups={{320,336,352,368,384,400,416,432,448,464,480,496,0,16,32,48,64,80,96,11..., dimensions={0} | all-to-all | bytes 557056 | tf_op jit(solution)/shard_map/all_to_all | solution.py:318
  20.6 0.8 %prefix.1 = (f32[32,16,128]{2,1,0:T(8,128)}, f32[32,128]{1,0:T(8,128)S(1)}) custom-call(f32[32,17,1,128]{3,2,1,0:T(1,128)S(1)} %all_to_all.25.members_ref), custom_call_target="tpu_custom_call" | custom-call | bytes 557056 | tf_op jit(solution)/shard_map/prefix/pallas_call | solution.py:291
  21.4 8.1 %all-to-all-start.1 = ((f32[32,16,128]{2,1,0:T(8,128)}), f32[32,16,128]{2,1,0:T(8,128)S(1)}, u32[]{:S(2)}, u32[]{:S(2)}) async-start(f32[32,16,128]{2,1,0:T(8,128)} %get-tuple-element.28), calls=%async_computation.1 | async-start | bytes 524288 | tf_op jit(solution)/shard_map/all_to_all | solution.py:318
  29.5 0.0 copy-done
  29.6 0.0 copy-done.1
  29.6 0.0 copy-done.3
  29.6 0.0 copy-done.5
  29.6 2.4 %local_attention.1 = (f32[512,512]{1,0:T(8,128)S(1)}, bf16[4,128,512]{2,1,0:T(8,128)(2,1)}, f32[1,512]{1,0:T(1,128)S(1)}) custom-call(bf16[512,512]{1,0:T(8,128)(2,1)S(1)} %copy-done.3, bf16[512,512]{1,0:T(8,128)(2,1)S(1)} %copy-done, bf16[512,512]{1,0:T(8,128)(2,1)S(1)} %copy-done.1, f32[8,512]{1,0:T(8,128)S(1)} %get-tuple-element.24.cum_ref, ...), custom_call_target="tpu_custom_call" | custom-call | flops 536870912 | bytes 3166208 | tf_op jit(solution)/shard_map/local_attention/pallas_call | solution.py:291
  32.0 1.7 %all-to-all-done.1 = f32[32,16,128]{2,1,0:T(8,128)S(1)} async-done(((f32[32,16,128]{2,1,0:T(8,128)}), f32[32,16,128]{2,1,0:T(8,128)S(1)}, u32[]{:S(2)}, u32[]{:S(2)}) %all-to-all-start.1) | async-done | bytes 262176 | tf_op jit(solution)/shard_map/all_to_all | solution.py:318
  33.7 0.0 copy-start.4
  33.7 0.0 copy-done.2
  33.7 0.7 attend.1
  34.4 17.9 %all_to_all.26.sums_ref = f32[16,8,128]{2,1,0:T(8,128)S(1)} all-to-all(f32[16,8,128]{2,1,0:T(8,128)S(1)} %get-tuple-element.29), channel_id=1, replica_groups={{10,11,12,13,14,15,0,1,2,3,4,5,6,7,8,9},{26,27,28,29,30,31,16,17,18,19,..., dimensions={0} | all-to-all | bytes 131072 | tf_op jit(solution)/shard_map/all_to_all | solution.py:318
  52.3 0.0 copy-done.4
  52.3 0.7 grad_states.1
  53.0 13.2 %all_to_all.27.members_ref = f32[32,16,128]{2,1,0:T(8,128)S(1)} all-to-all(f32[32,16,128]{2,1,0:T(8,128)S(1)} %get-tuple-element.33), channel_id=1, replica_groups={{320,336,352,368,384,400,416,432,448,464,480,496,0,16,32,48,64,80,96,11..., dimensions={0} | all-to-all | bytes 524288 | tf_op jit(solution)/shard_map/all_to_all | solution.py:318
  66.2 0.8 suffix.1
  67.0 8.2 %all-to-all-start.4 = ((f32[32,16,128]{2,1,0:T(8,128)}), f32[32,16,128]{2,1,0:T(8,128)S(1)}, u32[]{:S(2)}, u32[]{:S(2)}) async-start(f32[32,16,128]{2,1,0:T(8,128)} %get-tuple-element.40), calls=%async_computation.4 | async-start | bytes 524288 | tf_op jit(solution)/shard_map/all_to_all | solution.py:318
  75.2 1.0 %mix.1 = (bf16[4,512,512]{2,1,0:T(8,128)(2,1)S(1)}, f32[512,512]{1,0:T(8,128)S(1)}, bf16[512,512]{1,0:T(8,128)(2,1)S(1)}) custom-call(bf16[512,512]{1,0:T(8,128)(2,1)S(1)} %copy-done.3, bf16[512,512]{1,0:T(8,128)(2,1)S(1)} %copy-done, bf16[512,512]{1,0:T(8,128)(2,1)S(1)} %get-tuple-element.32.grad_ref, f32[8,512]{1,0:T(8,128)S(1)} %get-tuple-element.24.cum_ref, ...), custom_call_target="tpu_custom_call" | custom-call | flops 536870912 | bytes 5521920 | tf_op jit(solution)/shard_map/mix/pallas_call | solution.py:291
  76.2 3.0 %local_grads.1 = (bf16[512,512]{1,0:T(8,128)(2,1)}, bf16[512,512]{1,0:T(8,128)(2,1)S(1)}, bf16[512,512]{1,0:T(8,128)(2,1)S(1)}) custom-call(bf16[512,512]{1,0:T(8,128)(2,1)S(1)} %copy-done.3, bf16[512,512]{1,0:T(8,128)(2,1)S(1)} %copy-done, bf16[512,512]{1,0:T(8,128)(2,1)S(1)} %copy-done.1, bf16[512,512]{1,0:T(8,128)(2,1)S(1)} %get-tuple-element.36.grad_ref, ...), custom_call_target="tpu_custom_call" | custom-call | flops 1073741824 | bytes 6832128 | tf_op jit(solution)/shard_map/local_grads/pallas_call | solution.py:291
  79.2 0.1 all-to-all-done.4
  79.3 1.5 %add_carried.1 = (bf16[512,512]{1,0:T(8,128)(2,1)}, bf16[512,512]{1,0:T(8,128)(2,1)}) custom-call(bf16[512,512]{1,0:T(8,128)(2,1)S(1)} %copy-done, bf16[512,512]{1,0:T(8,128)(2,1)S(1)} %copy-done.1, f32[8,512]{1,0:T(8,128)S(1)} %get-tuple-element.24.cum_ref, f32[4,128,128]{2,1,0:T(8,128)S(1)} %bitcast.4, ...), custom_call_target="tpu_custom_call" | custom-call | flops 268435456 | bytes 3424256 | tf_op jit(solution)/shard_map/add_carried/pallas_call | solution.py:291
Async XLA Ops:
  0.6 28.9 %copy-start = (bf16[512,512]{1,0:T(8,128)(2,1)S(1)}, bf16[512,512]{1,0:T(8,128)(2,1)}, u32[]{:S(2)}) copy-start(bf16[512,512]{1,0:T(8,128)(2,1)} %keys_ref.7) | copy-start | bytes 1572868
  0.6 28.9 %copy-start.1 = (bf16[512,512]{1,0:T(8,128)(2,1)S(1)}, bf16[512,512]{1,0:T(8,128)(2,1)}, u32[]{:S(2)}) copy-start(bf16[512,512]{1,0:T(8,128)(2,1)} %values_ref.5) | copy-start | bytes 1572868
  0.7 28.9 %copy-start.3 = (bf16[512,512]{1,0:T(8,128)(2,1)S(1)}, bf16[512,512]{1,0:T(8,128)(2,1)}, u32[]{:S(2)}) copy-start(bf16[512,512]{1,0:T(8,128)(2,1)} %queries_ref.7) | copy-start | bytes 1572868
  0.7 28.9 %copy-start.5 = (f32[512]{0:T(512)S(1)}, f32[512]{0:T(512)}, u32[]{:S(2)}) copy-start(f32[512]{0:T(512)} %param.10) | copy-start | bytes 6148
  0.7 33.0 %copy-start.2 = (bf16[512,512]{1,0:T(8,128)(2,1)S(1)}, bf16[512,512]{1,0:T(8,128)(2,1)}, u32[]{:S(2)}) copy-start(bf16[512,512]{1,0:T(8,128)(2,1)} %upstream_ref.3) | copy-start | bytes 1572868
  21.4 12.3 %all-to-all-start.1 = ((f32[32,16,128]{2,1,0:T(8,128)}), f32[32,16,128]{2,1,0:T(8,128)S(1)}, u32[]{:S(2)}, u32[]{:S(2)}) async-start(f32[32,16,128]{2,1,0:T(8,128)} %get-tuple-element.28), calls=%async_computation.1 | async-start | bytes 524288 | tf_op jit(solution)/shard_map/all_to_all | solution.py:318
  33.7 18.6 %copy-start.4 = (bf16[4,128,512]{2,1,0:T(8,128)(2,1)S(1)}, bf16[4,128,512]{2,1,0:T(8,128)(2,1)}, u32[]{:S(2)}) copy-start(bf16[4,128,512]{2,1,0:T(8,128)(2,1)} %get-tuple-element.31.weighted_ref) | copy-start | bytes 1572868
  67.0 12.3 %all-to-all-start.4 = ((f32[32,16,128]{2,1,0:T(8,128)}), f32[32,16,128]{2,1,0:T(8,128)S(1)}, u32[]{:S(2)}, u32[]{:S(2)}) async-start(f32[32,16,128]{2,1,0:T(8,128)} %get-tuple-element.40), calls=%async_computation.4 | async-start | bytes 524288 | tf_op jit(solution)/shard_map/all_to_all | solution.py:318
